TPU v7x, 256 devices: a whole 4x4x8 slice. The times are simulated.
256 devices in a mesh: dp: 32 (over z, x), seq: 2 (over core), tensor: 4 (over y).
Axes of the slice: x: 4, y: 4, z: 8, core: 2. Of those that a mesh axis runs over, the one named last changes fastest.
Arguments:
- tokens: bfloat16 [32, 2048, 8192], P('dp', 'seq', 'tensor'), may hold values from -6 to 6
- input_map: bfloat16 [32, 2048, 512], P('dp', 'seq', 'tensor'), may hold values from -0.5 to 0.5
- output_map: bfloat16 [32, 2048, 512], P('dp', 'seq', 'tensor'), may hold values from -0.5 to 0.5
- log_decay: float32 [32, 128, 2048], P('dp', 'tensor', 'seq'), may hold values from -2 to 0, as said below
- step_size: float32 [32, 128, 2048], P('dp', 'tensor', 'seq'), may hold values from 0.05 to 0.2
- skip_gain: float32 [128], P('tensor'), may hold values from 0.5 to 1.5
- snapshots: bfloat16 [128, 128, 64, 128], P(('dp', 'seq'), 'tensor'), may hold values from -3 to 3
- first_snap: int32 [32], replicated, may hold values from 0 to 120
- prefix_kilo: int32 [32], replicated, may hold values from 1 to 8
- snap_slot: int32 [128], replicated, may hold values from 0 to 127, each once
Outputs:
- scan_out: bfloat16 [32, 2048, 8192], P('dp', ('seq', 'tensor'))
Inputs may be any that keep to these rules, and one draw needn't show every extreme that they name: A request's conversation has catalogue entries first_snap to first_snap + 7. Request r reloads catalogue entry first_snap[r] + prefix_kilo[r] - 1. `snap_slot`: each slot appears once; slot k is row k of snapshots. `log_decay`: strictly negative.
All inputs are finite; a program needn't handle non-finite values.
Results may differ from a plain program's by a relative error of at most 0.005.
Values may be sent and summed in bfloat16 or wider, within the bound.
A program may use at most 192 MiB of HBM per device.

v0:
```python
import jax
import jax.numpy as jnp
from jax import lax
from jax.sharding import PartitionSpec as P

HEAD_DIM = 64
STATE = 128
BLOCK = 128


def prefix(shard, axis, join, neutral):
    place = lax.axis_index(axis)
    gathered = jax.tree.map(
        lambda a, kind: lax.all_gather(a.astype(kind), axis), shard, (jnp.bfloat16, jnp.bfloat16)
    )
    state = jax.tree.map(lambda a, e: jnp.zeros_like(a) + jnp.asarray(e, a.dtype), shard, neutral)

    def one(hop, state):
        return join(
            state,
            jax.tree.map(
                lambda a, own: lax.dynamic_index_in_dim(a, hop, 0, False).astype(own.dtype),
                gathered,
                shard,
            ),
        )

    return lax.fori_loop(0, place, one, state)


def block_local(tokens_blk, input_blk, output_blk, decay_blk, step_blk):
    length = tokens_blk.shape[0]
    head_count = decay_blk.shape[0]
    groups = input_blk.shape[1] // STATE
    within_group = head_count // groups
    running = jnp.cumsum(decay_blk, axis=1)
    values = tokens_blk.reshape(length, groups, within_group, HEAD_DIM)
    inputs = input_blk.reshape(length, groups, STATE)
    outputs = output_blk.reshape(length, groups, STATE)
    scores = jnp.einsum("qgn,kgn->gqk", outputs, inputs, preferred_element_type=jnp.float32)
    later_position = lax.broadcasted_iota(jnp.int32, (length, length), 0)
    earlier = lax.broadcasted_iota(jnp.int32, (length, length), 1)
    spread = jnp.minimum(running[:, :, None] - running[:, None, :], 0.0)
    falloff = jnp.where(later_position >= earlier, jnp.exp(spread), 0.0) * step_blk[:, None, :]
    weights = (scores[:, None] * falloff.reshape(groups, within_group, length, length)).astype(
        jnp.bfloat16
    )
    inner_part = jnp.einsum("gkqs,sgkp->qgkp", weights, values, preferred_element_type=jnp.float32)
    ending = running[:, -1:]
    factor = (jnp.exp(ending - running) * step_blk).reshape(groups, within_group, length)
    scaled = (values * jnp.transpose(factor, (2, 0, 1))[..., None]).astype(jnp.bfloat16)
    state_add = jnp.einsum("qgkp,qgn->gkpn", scaled, inputs, preferred_element_type=jnp.float32)
    return (
        inner_part,
        state_add.reshape(head_count, HEAD_DIM, STATE),
        jnp.exp(ending[:, 0]),
        running,
    )


def combine(earlier, later_part):
    return (
        earlier[0] * later_part[0],
        later_part[0][:, :, None, None] * earlier[1] + later_part[1],
    )


def per_device(
    tokens,
    input_map,
    output_map,
    log_decay,
    step_size,
    skip_gain,
    snapshots,
    first_snap,
    prefix_kilo,
    snap_slot,
):
    local_reqs, local_len, feature_width = tokens.shape
    head_count = log_decay.shape[1]
    groups = input_map.shape[2] // STATE
    within_group = head_count // groups
    blocks = local_len // BLOCK
    seq_first = lax.axis_index("seq") == 0
    device_decays, summaries, inner_parts, start_states, reach_decays, runnings = (
        [],
        [],
        [],
        [],
        [],
        [],
    )
    request = 0
    pieces = (
        tokens[request].reshape(blocks, BLOCK, feature_width),
        input_map[request].reshape(blocks, BLOCK, groups * STATE),
        output_map[request].reshape(blocks, BLOCK, groups * STATE),
        jnp.transpose(log_decay[request].reshape(head_count, blocks, BLOCK), (1, 0, 2)),
        jnp.transpose(step_size[request].reshape(head_count, blocks, BLOCK), (1, 0, 2)),
    )

    def advance(carry, block_in):
        state_now, reach_decay = carry
        inner_part, state_add, block_fall, running = block_local(*block_in)
        carry_next = (block_fall[:, None, None] * state_now + state_add, reach_decay * block_fall)
        return (carry_next, (inner_part, state_now, reach_decay, running))

    start_carry = (
        jnp.zeros((head_count, HEAD_DIM, STATE), jnp.float32),
        jnp.ones((head_count,), jnp.float32),
    )
    (summary, device_decay), (inner_part, start_state, reach_decay, running) = lax.scan(
        advance, start_carry, pieces
    )
    device_decays.append(device_decay)
    summaries.append(summary)
    inner_parts.append(inner_part)
    start_states.append(start_state)
    reach_decays.append(reach_decay)
    runnings.append(running)
    decay_all = jnp.stack(device_decays)
    summary_all = jnp.stack(summaries)
    chosen = snap_slot[first_snap + prefix_kilo - 1]
    slots_here = snapshots.shape[0]
    seq_count = lax.axis_size("seq")
    dp_count = lax.axis_size("dp")
    piece_dim = HEAD_DIM // seq_count
    split_up = snapshots.reshape(slots_here, head_count, seq_count, piece_dim, STATE)
    split_up = jnp.transpose(split_up, (2, 0, 1, 3, 4))
    row_pieces = lax.all_to_all(split_up, "seq", split_axis=0, concat_axis=0, tiled=True)
    row_slots = row_pieces.reshape(seq_count * slots_here, head_count, piece_dim, STATE)
    row_size = seq_count * slots_here
    owner_row = chosen // row_size
    local_index = chosen % row_size
    picked = row_slots[local_index]
    mine = (owner_row == lax.axis_index("dp"))[:, None, None, None]
    outgoing = jnp.where(mine, picked, jnp.zeros_like(picked))
    outgoing = outgoing.reshape(dp_count, local_reqs, head_count, piece_dim, STATE)
    incoming = lax.all_to_all(outgoing, "dp", split_axis=0, concat_axis=0, tiled=True)
    my_pieces = jnp.sum(incoming.astype(jnp.float32), axis=0).astype(jnp.bfloat16)
    loaded = lax.all_gather(my_pieces, "seq", axis=2, tiled=True)
    prefix_state = loaded.astype(jnp.float32)
    single_element = jnp.where(
        seq_first, decay_all[:, :, None, None] * prefix_state + summary_all, summary_all
    )
    identity = (jnp.ones_like(decay_all), jnp.zeros_like(single_element))
    decay_before, state_before = prefix((decay_all, single_element), "seq", combine, identity)
    entering = state_before + jnp.where(seq_first, prefix_state, 0.0)
    request = 0
    block_states = (
        reach_decays[request][:, :, None, None] * entering[request][None] + start_states[request]
    )
    output_wide = output_map[request].reshape(blocks, BLOCK, groups, STATE).astype(jnp.float32)
    carried = jnp.einsum(
        "bqgn,bgkpn->bqgkp",
        output_wide,
        block_states.reshape(blocks, groups, within_group, HEAD_DIM, STATE),
        precision=lax.Precision.HIGHEST,
    )
    growth = jnp.transpose(
        jnp.exp(runnings[request]).reshape(blocks, groups, within_group, BLOCK), (0, 3, 1, 2)
    )[..., None]
    values = tokens[request].reshape(blocks, BLOCK, groups, within_group, HEAD_DIM)
    mixed_out = (
        inner_parts[request]
        + carried * growth
        + values * skip_gain.reshape(groups, within_group)[None, None, :, :, None]
    )
    results = [mixed_out.reshape(local_len, feature_width).astype(jnp.bfloat16)]
    stacked = jnp.stack(results)
    return lax.all_to_all(stacked, "tensor", split_axis=1, concat_axis=2, tiled=True)


def solution(mesh):
    placed = (
        P("dp", "seq", "tensor"),
        P("dp", "seq", "tensor"),
        P("dp", "seq", "tensor"),
        P("dp", "tensor", "seq"),
        P("dp", "tensor", "seq"),
        P("tensor"),
        P(("dp", "seq"), "tensor", None, None),
        P(),
        P(),
        P(),
    )
    return jax.shard_map(
        per_device,
        mesh=mesh,
        in_specs=placed,
        out_specs=P("dp", ("seq", "tensor"), None),
        check_vma=False,
    )
```

profile of v0, /device:TPU:1, one launch (start us, length us, event | category | flops | bytes accessed | tf_op | source)
XLA Modules:
  0.0 440.3 jit_solution(743266211985535437)
XLA Ops:
  6.5 2.3 copy.40
  8.8 6.8 %all-to-all-start = ((bf16[2,2,32,32,128]{4,3,2,1,0:T(8,128)(2,1)}), bf16[2,2,32,32,128]{4,3,2,1,0:T(8,128)(2,1)S(1)}, u32[]{:S(2)}, u32[]{:S(2)}) async-start(bf16[2,2,32,32,128]{4,3,2,1,0:T(8,128)(2,1)} %copy.40), calls=%async_computation | async-start | bytes 2097152 | tf_op jit(solution)/shard_map/all_to_all | solution.py:131
  17.4 4.9 %gather_fusion.1 = bf16[32,32,32,128]{3,2,1,0:T(8,128)(2,1)} fusion(bf16[4,32,32,128]{3,2,1,0:T(8,128)(2,1)S(1)} %bitcast.161, s32[1024]{0:T(1024)S(1)} %pad_clamp_fusion), kind=kCustom, calls=%fused_computation.1 | custom fusion | bytes 16777344 | tf_op jit(solution)/shard_map/gather | solution.py:136
  22.3 7.2 %fusion.26 = bf16[32,1,32,32,128]{4,3,2,1,0:T(8,128)(2,1)} fusion(bf16[32,32,32,128]{3,2,1,0:T(8,128)(2,1)} %gather_fusion.1, pred[32]{0:T(512)(128)(4,1)S(1)} %fusion.39), kind=kLoop, calls=%fused_computation.45 | loop fusion | flops 4194304 | bytes 16777248 | tf_op jit(solution)/shard_map/jit(_where)/select_n | solution.py:138
  29.5 9.6 %all-to-all-start.1 = ((bf16[32,1,32,32,128]{4,3,2,1,0:T(8,128)(2,1)}), bf16[32,1,32,32,128]{4,3,2,1,0:T(8,128)(2,1)}, u32[]{:S(2)}, u32[]{:S(2)}) async-start(bf16[32,1,32,32,128]{4,3,2,1,0:T(8,128)(2,1)} %fusion.26), calls=%async_computation.1 | async-start | bytes 16777216 | tf_op jit(solution)/shard_map/all_to_all | solution.py:140
  39.3 57.3 %while.34 = (s32[]{:T(128)}, f32[32,64,128]{2,1,0:T(8,128)S(1)}, f32[32]{0:T(128)S(1)}, f32[8,128,1,32,64]{1,4,3,2,0:T(8,128)}, f32[8,32,64,128]{3,2,1,0:T(8,128...) while((s32[]{:T(128)}, f32[32,64,128]{2,1,0:T(8,128)S(1)}, ...), condition=%wide.region_2.3_spmd.clone, body=%wide.region_0.2_spmd.clone.sunk | while | flops 143937600 | bytes 9933229 | solution.py:113
  39.6 0.9 fusion.59
  40.5 1.1 constant_dynamic-slice_fusion.5
  41.9 2.0 fusion.60
  44.3 1.0 bitcast_dynamic-update-slice_fusion.5
  45.3 1.1 convolution_add_fusion.2
  46.8 0.9 fusion.59
  47.7 1.1 constant_dynamic-slice_fusion.5
  49.1 1.9 fusion.60
  51.4 1.1 bitcast_dynamic-update-slice_fusion.5
  52.5 1.1 convolution_add_fusion.2
  54.0 0.9 fusion.59
  54.8 1.1 constant_dynamic-slice_fusion.5
  56.3 1.9 fusion.60
  58.6 1.1 bitcast_dynamic-update-slice_fusion.5
  59.7 1.1 convolution_add_fusion.2
  61.1 0.9 fusion.59
  62.0 1.1 constant_dynamic-slice_fusion.5
  63.4 1.9 fusion.60
  65.7 1.1 bitcast_dynamic-update-slice_fusion.5
  66.8 1.1 convolution_add_fusion.2
  68.2 0.9 fusion.59
  69.1 1.1 constant_dynamic-slice_fusion.5
  70.5 2.0 fusion.60
  72.9 1.1 bitcast_dynamic-update-slice_fusion.5
  74.0 1.1 convolution_add_fusion.2
  75.4 0.9 fusion.59
  76.3 1.1 constant_dynamic-slice_fusion.5
  77.7 1.9 fusion.60
  80.1 1.1 bitcast_dynamic-update-slice_fusion.5
  81.1 1.1 convolution_add_fusion.2
  82.6 0.9 fusion.59
  83.5 1.1 constant_dynamic-slice_fusion.5
  84.9 1.9 fusion.60
  87.2 1.1 bitcast_dynamic-update-slice_fusion.5
  88.3 1.1 convolution_add_fusion.2
  89.8 0.9 fusion.59
  90.7 1.1 constant_dynamic-slice_fusion.5
  92.1 1.9 fusion.60
  94.4 1.1 bitcast_dynamic-update-slice_fusion.5
  95.5 1.1 convolution_add_fusion.2
  96.6 130.5 %all-to-all-done.1 = bf16[32,1,32,32,128]{4,3,2,1,0:T(8,128)(2,1)} async-done(((bf16[32,1,32,32,128]{4,3,2,1,0:T(8,128)(2,1)}), bf16[32,1,32,32,128]{4,3,2,1,0:T(8,128)(2,1)}, u32[]{:S(2)}, u32[]{:S(2)}) %all-to-all-start.1) | async-done | bytes 8388640 | tf_op jit(solution)/shard_map/all_to_all | solution.py:140
  227.1 4.8 %reduce_sum.14 = bf16[32,32,128]{2,1,0:T(8,128)(2,1)S(1)} reduce(bf16[32,1,32,32,128]{4,3,2,1,0:T(8,128)(2,1)} %all-to-all-done.1, bf16[]{:T(256)} %constant.103.clone.1), dimensions={0,1}, to_apply=%region_3.4 | reduce | flops 4063232 | bytes 8650754 | tf_op jit(solution)/shard_map/reduce_sum | solution.py:141
  231.9 3.2 all-gather.1
  235.1 1.0 fusion.36
  236.2 19.9 %copy.45 = f32[1,1024,2048]{1,0,2:T(1,128)} copy(bf16[1,1024,2048]{2,1,0:T(8,128)(2,1)} %bitcast.170) | data formatting | bytes 12582912 | tf_op jit(solution)/shard_map/convert_element_type | solution.py:168
  257.7 2.5 all-reduce
  260.4 1.5 while.33
  260.5 1.3 convert_add_fusion.2
  262.2 13.6 %fusion.25 = bf16[8,128,1,32,64]{1,4,3,0,2:T(8,128)(2,1)} fusion(f32[8,128,1,32,64]{1,4,3,2,0:T(8,128)} %get-tuple-element.116, f32[8,128,1,32,64]{1,0,2,4,3:T(8,128)} %bitcast.163, f32[32]{0:T(128)S(1)} %copy-done.5, f32[8,128,32]{1,2,0:T(8,128)S(1)} %exponential_bitcast_fusion, bf16[8,128,128,1]{2,1,3,0:T(8,128)(2,1)S(1)} %bitcast.176, ...), kind=kOutput, calls=%fused_computation.43 | convolution fusion | flops 3235905536 | bytes 30803072 | tf_op jit(solution)/shard_map/bqgn,bgkpn->bqgkp/dot_general | solution.py:155
  275.8 12.8 %copy.52 = bf16[8,128,1,32,64]{4,3,1,0,2:T(8,128)(2,1)} copy(bf16[8,128,1,32,64]{1,4,3,0,2:T(8,128)(2,1)} %fusion.25) | data formatting | bytes 8388608 | tf_op jit(solution)/shard_map/convert_element_type | solution.py:170
  288.6 28.5 %reshape.289 = bf16[1,1024,2048]{2,0,1:T(2,128)(2,1)} reshape(bf16[8,128,1,32,64]{4,3,1,0,2:T(8,128)(2,1)} %copy.52) | data formatting | bytes 8388608 | tf_op jit(solution)/shard_map/convert_element_type | solution.py:170
  317.7 27.2 %reduce.4 = bf16[1024,2048]{1,0:T(8,128)(2,1)} reduce(bf16[1024,1,2048]{2,1,0:T(2,128)(2,1)} %bitcast.166, bf16[]{:T(256)} %broadcast.212), dimensions={1}, to_apply=%bitcast.122.reduce_sub_computation | reduce | bytes 8388610
  344.9 6.2 %reshape.291 = bf16[4,2,262144]{2,1,0:T(2,128)(2,1)} reshape(bf16[1024,2048]{1,0:T(8,128)(2,1)} %reduce.4) | data formatting | bytes 8388608
  351.2 54.3 %all_to_all.28 = bf16[4,2,262144]{2,1,0:T(2,128)(2,1)} all-to-all(bf16[4,2,262144]{2,1,0:T(2,128)(2,1)} %reshape.291), channel_id=1, replica_groups=mesh['dp'=32,'seq'=2,'tensor'=4] {'tensor'}, dimensions={0} | all-to-all | bytes 8388608 | tf_op jit(solution)/shard_map/all_to_all | solution.py:172
  405.5 7.4 %reshape.292 = bf16[1024,1,2048]{2,1,0:T(2,128)(2,1)} reshape(bf16[4,2,262144]{2,1,0:T(2,128)(2,1)} %all_to_all.28) | data formatting | bytes 8388608
  412.9 8.0 %copy.57 = bf16[1,1024,2048]{2,1,0:T(8,128)(2,1)} copy(bf16[1,1024,2048]{2,0,1:T(2,128)(2,1)} %bitcast.165) | data formatting | bytes 8388608
  420.9 6.2 %copy.49 = bf16[1,256,4,2048]{1,3,2,0:T(8,128)(2,1)} copy(bf16[1,256,4,2048]{3,1,2,0:T(8,128)(2,1)} %bitcast.167) | data formatting | bytes 8388608 | tf_op jit(solution)/shard_map/all_to_all | solution.py:172
  427.2 6.3 %copy.50 = bf16[1,256,8192]{2,1,0:T(8,128)(2,1)} copy(bf16[1,256,8192]{1,2,0:T(8,128)(2,1)} %bitcast.168) | data formatting | bytes 8388608 | tf_op jit(solution)/shard_map/all_to_all | solution.py:172
  (114 shorter events, 12.0 us)
Async XLA Ops:
  6.5 9.8 %copy-start = (s32[128]{0:T(128)S(1)}, s32[128]{0:T(128)}, u32[]{:S(2)}) copy-start(s32[128]{0:T(128)} %param.23) | copy-start | bytes 1540
  8.8 8.6 %all-to-all-start = ((bf16[2,2,32,32,128]{4,3,2,1,0:T(8,128)(2,1)}), bf16[2,2,32,32,128]{4,3,2,1,0:T(8,128)(2,1)S(1)}, u32[]{:S(2)}, u32[]{:S(2)}) async-start(bf16[2,2,32,32,128]{4,3,2,1,0:T(8,128)(2,1)} %copy.40), calls=%async_computation | async-start | bytes 2097152 | tf_op jit(solution)/shard_map/all_to_all | solution.py:131
  29.5 9.7 %copy-start.3 = (f32[1,32,1024]{2,1,0:T(8,128)S(1)}, f32[1,32,1024]{2,1,0:T(8,128)}, u32[]{:S(2)}) copy-start(f32[1,32,1024]{2,1,0:T(8,128)} %param.17) | copy-start | bytes 393220
  29.5 9.7 %copy-start.4 = (f32[1,32,1024]{2,1,0:T(8,128)S(1)}, f32[1,32,1024]{2,1,0:T(8,128)}, u32[]{:S(2)}) copy-start(f32[1,32,1024]{2,1,0:T(8,128)} %param.18) | copy-start | bytes 393220
  29.5 9.8 %copy-start.2 = (bf16[1,1024,128]{2,1,0:T(8,128)(2,1)S(1)}, bf16[1,1024,128]{2,1,0:T(8,128)(2,1)}, u32[]{:S(2)}) copy-start(bf16[1,1024,128]{2,1,0:T(8,128)(2,1)} %param.16) | copy-start | bytes 786436
  29.5 197.6 %all-to-all-start.1 = ((bf16[32,1,32,32,128]{4,3,2,1,0:T(8,128)(2,1)}), bf16[32,1,32,32,128]{4,3,2,1,0:T(8,128)(2,1)}, u32[]{:S(2)}, u32[]{:S(2)}) async-start(bf16[32,1,32,32,128]{4,3,2,1,0:T(8,128)(2,1)} %fusion.26), calls=%async_computation.1 | async-start | bytes 16777216 | tf_op jit(solution)/shard_map/all_to_all | solution.py:140
  39.1 221.2 %all-gather.5.cloned.1.call-start = ((), (), s32[]{:S(2)}) async-start(), calls=%async_computation.3 | async-start | bytes 1572864 | tf_op jit(solution)/shard_map/all_gather | solution.py:14
  231.9 24.2 %copy-start.6 = (u32[256]{0:T(256)S(1)}, u32[256]{0:T(256)}, u32[]{:S(2)}) copy-start(u32[256]{0:T(256)} %constant.112) | copy-start | bytes 3076
  260.3 1.9 copy-start.5
  420.9 12.6 %copy-start.1 = (s32[128]{0:T(128)S(1)}, s32[128]{0:T(128)}, u32[]{:S(2)}) copy-start(s32[128]{0:T(128)} %param.23) | copy-start | bytes 1540
Sparse Core Ops, SparseCore 0:
  236.3 19.4 all-gather.4
where the time goes:
time: 448 us; the launch traced here: 440 us
  waiting for transfers between devices  131 us (29%)
  local copies, waits for them, and re-layouts  118 us (26%)
  blocking collectives  60 us (13%)
  other arithmetic  55 us (12%)
  matrix products  44.8 us (10%)
  starting transfers between devices  16.4 us (4%)
  between operations  14.3 us (3%)
    all_to_all x1, waiting for transfers between devices, per_device(): lax.all_to_all(outgoing, 'dp', split_axis=0, concat_axis=0, tiled=True)  130 us
    all_to_all x1, blocking collectives, per_device(): lax.all_to_all(stacked, 'tensor', split_axis=1, concat_axis=2, tiled=True)  54.3 us
    convert_element_type x2, local copies, waits for them, and re-layouts, per_device(): results = [mixed_out.reshape(local_len, feature_width).astype(jnp.bfloat16)]  41.3 us
    unnamed x3, other arithmetic  27.2 us
    unnamed x23, local copies, waits for them, and re-layouts  23.3 us
    convert_element_type x1, local copies, waits for them, and re-layouts, per_device(): values * skip_gain.reshape(groups, within_group)[None, None, :, :, None]  19.9 us
    dot_general x8, matrix products, block_local(): jnp.einsum('gkqs,sgkp->qgkp', weights, values, preferred_element_type=jnp...  15.5 us
    dot_general x1, matrix products, per_device(): jnp.einsum('bqgn,bgkpn->bqgkp', output_wide, block_states.reshape(blocks,...  13.6 us
  transfers between devices with their start and end apart: 3, of which 2 were waited for; matrix products, arithmetic and copies ran while one was open for 18% of the time, Pallas kernels for 0%

commit v1 on v0

v1 whole, which is shorter than its diff:
```python
import functools

import jax
import jax.numpy as jnp
from jax import lax
from jax.experimental import pallas as pl
from jax.experimental.pallas import tpu as pltpu
from jax.sharding import PartitionSpec as P

HEAD_DIM = 64
STATE = 128
BLOCK = 128
CHUNK = 8 * HEAD_DIM
LOG2E = 1.4426950408889634
MESH = pl.DeviceIdType.MESH
F32 = jnp.float32
BF16 = jnp.bfloat16


def prepare(blocks, b_ref, c_ref, ld_ref, dt_ref, gain_ref, sm, bt, run_t, urow, fac, rows_e):
    heads = ld_ref.shape[0]
    width = heads * HEAD_DIM
    row = lax.broadcasted_iota(jnp.int32, (BLOCK, BLOCK), 0)
    col = lax.broadcasted_iota(jnp.int32, (BLOCK, BLOCK), 1)
    upto = (row <= col).astype(F32)
    ends = []
    for b in range(blocks):
        at = pl.ds(b * BLOCK, BLOCK)
        run = jnp.dot(
            ld_ref[:, at], upto, precision=lax.Precision.HIGHEST, preferred_element_type=F32
        )
        run = run * LOG2E
        step = dt_ref[:, at]
        end = run[:, BLOCK - 1 :]
        urow[:, at] = run - jnp.log2(step)
        fac[:, at] = jnp.exp2(end - run) * step
        padded = jnp.concatenate([run, jnp.zeros((BLOCK - heads, BLOCK), F32)], axis=0)
        turned = padded.T
        run_t[at, :] = turned
        ends.append(turned[BLOCK - 1 :, :])
        inputs = b_ref[at, :]
        scores = lax.dot_general(
            c_ref[at, :], inputs, (((1,), (1,)), ((), ())), preferred_element_type=F32
        )
        sm[at, :] = jnp.where(row >= col, scores, 0.0)
        bt[at, :] = inputs.astype(F32).T
    stacked = jnp.concatenate(ends + [gain_ref[...]], axis=0)
    pad = (-stacked.shape[0]) % 8
    if pad:
        stacked = jnp.concatenate([stacked, jnp.zeros((pad, BLOCK), F32)], axis=0)
    spot = lax.broadcasted_iota(jnp.int32, (BLOCK, width), 0)
    head = lax.broadcasted_iota(jnp.int32, (BLOCK, width), 1) // HEAD_DIM
    spread = (spot == head).astype(F32)
    wide = jnp.dot(stacked, spread, precision=lax.Precision.HIGHEST, preferred_element_type=F32)
    reach = jnp.zeros((1, width), F32)
    for b in range(blocks):
        end = wide[b : b + 1, :]
        rows_e[b] = jnp.broadcast_to(jnp.exp2(end), (8, width))
        rows_e[blocks + 1 + b] = jnp.broadcast_to(jnp.exp2(reach), (8, width))
        reach = reach + end
    rows_e[blocks] = jnp.broadcast_to(wide[blocks : blocks + 1, :], (8, width))
    rows_e[2 * blocks + 1] = jnp.broadcast_to(jnp.exp2(reach), (8, width))


def local_chunk(
    blocks, k, x_ref, c_ref, sm, bt, run_t, urow, fac, rows_e, state, summary, acc, growth
):
    cols = pl.ds(pl.multiple_of(k * CHUNK, CHUNK), CHUNK)
    octet = pl.ds(pl.multiple_of(k * 8, 8), 8)
    pair_width = 2 * HEAD_DIM
    first = lax.broadcasted_iota(jnp.int32, (1, pair_width), 1) < HEAD_DIM
    keep0 = jnp.where(first, 1.0, 0.0).astype(BF16)
    keep1 = jnp.where(first, 0.0, 1.0).astype(BF16)
    state[...] = jnp.zeros_like(state)

    def one(b, _):
        at = pl.ds(pl.multiple_of(b * BLOCK, BLOCK), BLOCK)
        turned = pltpu.roll(run_t[at, :], lax.rem(BLOCK - 8 * k, BLOCK), 1)
        u = urow[octet, at]
        f = fac[octet, at]
        carried = jnp.dot(c_ref[at, :], state[...].astype(BF16), preferred_element_type=F32)
        for j in range(CHUNK // pair_width):
            mine = slice(j * pair_width, (j + 1) * pair_width)
            here = pl.ds(pl.multiple_of(k * CHUNK + j * pair_width, pair_width), pair_width)
            h0, h1 = slice(2 * j, 2 * j + 1), slice(2 * j + 1, 2 * j + 2)
            scores = sm[at, :]
            back = bt[at, :]
            run0 = jnp.broadcast_to(turned[:, h0], (BLOCK, BLOCK))
            run1 = jnp.broadcast_to(turned[:, h1], (BLOCK, BLOCK))
            w0 = (scores * jnp.exp2(jnp.minimum(run0 - u[h0], 64.0))).astype(BF16)
            w1 = (scores * jnp.exp2(jnp.minimum(run1 - u[h1], 64.0))).astype(BF16)
            b0 = (back * f[h0]).astype(BF16)
            b1 = (back * f[h1]).astype(BF16)
            x = x_ref[at, here]
            left = jnp.concatenate(
                [jnp.concatenate([w0, w1], axis=1), jnp.concatenate([b0, b1], axis=1)], axis=0
            )
            right = jnp.concatenate([x * keep0, x * keep1], axis=0)
            both = jnp.dot(left, right, preferred_element_type=F32)
            grown = jnp.exp2(jnp.where(first, run0, run1))
            acc[at, here] = (
                both[:BLOCK]
                + grown * carried[:, mine]
                + x.astype(F32) * rows_e[blocks, :, here][0:1, :]
            )
            growth[at, here] = grown * rows_e[blocks + 1 + b, :, here][0:1, :]
            state[:, mine] = rows_e[b, :, here][0:1, :] * state[:, mine] + both[BLOCK:]
        return 0

    lax.fori_loop(0, blocks, one, 0, unroll=2)
    summary[:, cols] = state[...].astype(BF16)


def kernel(
    blocks,
    ranks,
    x_ref,
    b_ref,
    c_ref,
    ld_ref,
    dt_ref,
    gain_ref,
    s0_ref,
    o_ref,
    sm,
    bt,
    run_t,
    urow,
    fac,
    rows_e,
    state,
    summary,
    acc,
    growth,
    staged,
    sum_in,
    decay_in,
    sib_send,
    sib_recv,
    y_send,
    y_recv,
    own_sem,
):
    dp, core, y = lax.axis_index("dp"), lax.axis_index("seq"), lax.axis_index("tensor")
    sibling = (dp, 1 - core, y)
    quarter = blocks * BLOCK // ranks
    width = x_ref.shape[1]
    chunks = width // CHUNK

    def peer(step):
        return (dp, core, lax.rem(y + step, ranks))

    barrier = pltpu.get_barrier_semaphore()
    pl.semaphore_signal(barrier, inc=1, device_id=sibling, device_id_type=MESH)
    for step in range(1, ranks):
        pl.semaphore_signal(barrier, inc=1, device_id=peer(step), device_id_type=MESH)
    pl.semaphore_wait(barrier, ranks)

    prepare(blocks, b_ref, c_ref, ld_ref, dt_ref, gain_ref, sm, bt, run_t, urow, fac, rows_e)
    decay_copy = pltpu.make_async_remote_copy(
        src_ref=rows_e.at[2 * blocks + 1],
        dst_ref=decay_in,
        send_sem=sib_send.at[0],
        recv_sem=sib_recv.at[0],
        device_id=sibling,
        device_id_type=MESH,
    )
    decay_copy.start()

    def run_chunk(k, _):
        local_chunk(
            blocks, k, x_ref, c_ref, sm, bt, run_t, urow, fac, rows_e, state, summary, acc, growth
        )
        return 0

    lax.fori_loop(0, chunks, run_chunk, 0)
    sum_copy = pltpu.make_async_remote_copy(
        src_ref=summary,
        dst_ref=sum_in,
        send_sem=sib_send.at[1],
        recv_sem=sib_recv.at[1],
        device_id=sibling,
        device_id_type=MESH,
    )
    sum_copy.start()
    decay_copy.wait()
    sum_copy.wait()
    later = core == 1

    def y_copy(k, step):
        cols = pl.ds(pl.multiple_of(k * CHUNK, CHUNK), CHUNK)
        there = pl.ds(pl.multiple_of(y * width + k * CHUNK, CHUNK), CHUNK)
        rows = pl.ds(pl.multiple_of(lax.rem(y + step, ranks) * quarter, quarter), quarter)
        if step == 0:
            return pltpu.make_async_copy(staged.at[rows, cols], o_ref.at[:, there], own_sem.at[k])
        return pltpu.make_async_remote_copy(
            src_ref=staged.at[rows, cols],
            dst_ref=o_ref.at[:, there],
            send_sem=y_send.at[k, step - 1],
            recv_sem=y_recv.at[k, step - 1],
            device_id=peer(step),
            device_id_type=MESH,
        )

    def finish(k, _):
        cols = pl.ds(pl.multiple_of(k * CHUNK, CHUNK), CHUNK)
        decay = jnp.where(later, decay_in[0:1, cols], 1.0)
        earlier = jnp.where(later, sum_in[:, cols].astype(F32), 0.0).astype(BF16)
        begin = s0_ref[cols, :]
        for step in (2, 1, 3, 0):
            rows = pl.ds(pl.multiple_of(lax.rem(y + step, ranks) * quarter, quarter), quarter)
            c = c_ref[rows, :]
            mixed = decay * lax.dot_general(
                c, begin, (((1,), (1,)), ((), ())), preferred_element_type=F32
            ) + jnp.dot(c, earlier, preferred_element_type=F32)
            staged[rows, cols] = (acc[rows, cols] + growth[rows, cols] * mixed).astype(BF16)
            y_copy(k, step).start()
        return 0

    lax.fori_loop(0, chunks, finish, 0)

    def drain(k, _):
        for step in range(ranks):
            y_copy(k, step).wait()
        return 0

    lax.fori_loop(0, chunks, drain, 0)


def copy_kernel(parts, in_ref, out_ref, held, in_sem, out_sem):
    rows = in_ref.shape[0] // parts

    def part(i):
        return pl.ds(i * rows, rows)

    reads = [
        pltpu.make_async_copy(in_ref.at[part(i)], held.at[part(i)], in_sem.at[i])
        for i in range(parts)
    ]
    writes = [
        pltpu.make_async_copy(held.at[part(i)], out_ref.at[part(i)], out_sem.at[i])
        for i in range(parts)
    ]
    for read in reads:
        read.start()
    for read, write in zip(reads, writes):
        read.wait()
        write.start()
    for write in writes:
        write.wait()


def start_states(snapshots, first_snap, prefix_kilo, snap_slot):
    slots_here, heads = snapshots.shape[:2]
    row_size = 2 * slots_here
    dp_count = lax.axis_size("dp")
    spread = lax.all_to_all(snapshots, "dp", split_axis=1, concat_axis=0, tiled=True)
    chosen = snap_slot[first_snap + prefix_kilo - 1]
    within = chosen % row_size
    mine = within // slots_here == lax.axis_index("seq")
    picked = spread[(chosen // row_size) * slots_here + within % slots_here]
    picked = jnp.where(mine[:, None, None, None], picked, jnp.zeros_like(picked))
    got = lax.all_to_all(picked, "dp", split_axis=0, concat_axis=1, tiled=True)
    del heads, dp_count
    return lax.psum(got, "seq")[0]


def per_device(
    tokens,
    input_map,
    output_map,
    log_decay,
    step_size,
    skip_gain,
    snapshots,
    first_snap,
    prefix_kilo,
    snap_slot,
):
    length, width = tokens.shape[1:]
    heads = log_decay.shape[1]
    blocks = length // BLOCK
    ranks = lax.axis_size("tensor")
    chunks = width // CHUNK
    begin = start_states(snapshots, first_snap, prefix_kilo, snap_slot)
    gain = jnp.pad(skip_gain, (0, BLOCK - heads)).reshape(1, BLOCK)
    out_shape = (length // ranks, width * ranks)
    vmem = pl.BlockSpec(memory_space=pltpu.VMEM)
    mixed = pl.pallas_call(
        functools.partial(kernel, blocks, ranks),
        out_shape=jax.ShapeDtypeStruct(out_shape, BF16),
        in_specs=[vmem] * 7,
        out_specs=pl.BlockSpec(memory_space=pl.ANY),
        scratch_shapes=[
            pltpu.VMEM((length, BLOCK), F32),
            pltpu.VMEM((length, BLOCK), F32),
            pltpu.VMEM((length, BLOCK), F32),
            pltpu.VMEM((heads, length), F32),
            pltpu.VMEM((heads, length), F32),
            pltpu.VMEM((2 * blocks + 2, 8, width), F32),
            pltpu.VMEM((STATE, CHUNK), F32),
            pltpu.VMEM((STATE, width), BF16),
            pltpu.VMEM((length, width), F32),
            pltpu.VMEM((length, width), F32),
            pltpu.VMEM((length, width), BF16),
            pltpu.VMEM((STATE, width), BF16),
            pltpu.VMEM((8, width), F32),
            pltpu.SemaphoreType.DMA((2,)),
            pltpu.SemaphoreType.DMA((2,)),
            pltpu.SemaphoreType.DMA((chunks, ranks - 1)),
            pltpu.SemaphoreType.DMA((chunks, ranks - 1)),
            pltpu.SemaphoreType.DMA((chunks,)),
        ],
        compiler_params=pltpu.CompilerParams(
            collective_id=0, has_side_effects=True, vmem_limit_bytes=56 * 2**20
        ),
        name="scan_and_send",
    )(
        tokens[0],
        input_map[0],
        output_map[0],
        log_decay[0],
        step_size[0],
        gain,
        begin.reshape(width, STATE),
    )
    parts = 4
    result = pl.pallas_call(
        functools.partial(copy_kernel, parts),
        out_shape=jax.ShapeDtypeStruct(out_shape, BF16),
        in_specs=[pl.BlockSpec(memory_space=pl.ANY)],
        out_specs=pl.BlockSpec(memory_space=pl.ANY),
        scratch_shapes=[
            pltpu.VMEM(out_shape, BF16),
            pltpu.SemaphoreType.DMA((parts,)),
            pltpu.SemaphoreType.DMA((parts,)),
        ],
        compiler_params=pltpu.CompilerParams(vmem_limit_bytes=16 * 2**20),
        name="place_result",
    )(mixed)
    return result[None]


def solution(mesh):
    placed = (
        P("dp", "seq", "tensor"),
        P("dp", "seq", "tensor"),
        P("dp", "seq", "tensor"),
        P("dp", "tensor", "seq"),
        P("dp", "tensor", "seq"),
        P("tensor"),
        P(("dp", "seq"), "tensor", None, None),
        P(),
        P(),
        P(),
    )
    return jax.shard_map(
        per_device,
        mesh=mesh,
        in_specs=placed,
        out_specs=P("dp", ("seq", "tensor"), None),
        check_vma=False,
    )
```

time: 448 us -> 181 us (0.40); the launches traced: 440 us -> 180 us
  local copies, waits for them, and re-layouts: 118 us -> 6.4 us
  waiting for transfers between devices: 131 us -> 54.6 us
  Pallas kernels: 0 us -> 72.7 us
  other arithmetic: 55 us -> 0.17 us
  matrix products: 44.8 us -> 0 us
  blocking collectives: 60 us -> 21.2 us
  starting transfers between devices: 16.4 us -> 11.9 us
    all_to_all x2 -> x1, waiting for transfers between devices: 131 us -> 25.3 us  [start_states(): lax.all_to_all(snapshots, 'dp', split_axis=1, concat_axis=0, tiled=True)]
    pallas_call x0 -> x2, Pallas kernels: none -> 72.7 us  [the longest x1 70.3 us: per_device(): pl.pallas_call(functools.partial(kernel, blocks, ranks), out_shape=jax.Sh...]
    convert_element_type x3 -> x0, local copies, waits for them, and re-layouts: 61.2 us -> none  [the longest x2 41.3 us: per_device(): results = [mixed_out.reshape(local_len, feature_width).astype(jnp.bfloat16)]]
    dot_general x25 -> x0, matrix products: 44.8 us -> none  [the longest x8 15.5 us: block_local(): jnp.einsum('gkqs,sgkp->qgkp', weights, values, preferred_element_type=jnp...]
    all_to_all x1, blocking collectives: 54.3 us -> 21.2 us  [start_states(): got = lax.all_to_all(picked, 'dp', split_axis=0, concat_axis=1, tiled=True)]
    psum x0 -> x1, waiting for transfers between devices: none -> 29.3 us  [start_states(): return lax.psum(got, 'seq')[0]]
    unnamed x3 -> x0, other arithmetic: 27.2 us -> none
    unnamed x23 -> x11, local copies, waits for them, and re-layouts: 23.3 us -> 4.54 us
  transfers between devices with their start and end apart: 3 -> 2, of which waited for: 2 -> 2; matrix products, arithmetic and copies ran while one was open for 18% -> 1% of each run, Pallas kernels for 0% -> 0%
where the time goes in v1:
time: 181 us; the launch traced here: 180 us
  Pallas kernels  72.7 us (40%)
  waiting for transfers between devices  54.6 us (30%)
  blocking collectives  21.2 us (12%)
  between operations  13.5 us (7%)
  starting transfers between devices  11.9 us (7%)
  local copies, waits for them, and re-layouts  6.4 us (4%)
    pallas_call x1, Pallas kernels, per_device(): pl.pallas_call(functools.partial(kernel, blocks, ranks), out_shape=jax.Sh...  70.3 us
    psum x1, waiting for transfers between devices, start_states(): return lax.psum(got, 'seq')[0]  29.3 us
    all_to_all x1, waiting for transfers between devices, start_states(): lax.all_to_all(snapshots, 'dp', split_axis=1, concat_axis=0, tiled=True)  25.3 us
    all_to_all x1, blocking collectives, start_states(): got = lax.all_to_all(picked, 'dp', split_axis=0, concat_axis=1, tiled=True)  21.2 us
    all_to_all x1, starting transfers between devices, start_states(): lax.all_to_all(snapshots, 'dp', split_axis=1, concat_axis=0, tiled=True)  11.9 us
    unnamed x11, local copies, waits for them, and re-layouts  4.54 us
  transfers between devices with their start and end apart: 2, of which 2 were waited for; matrix products, arithmetic and copies ran while one was open for 1% of the time, Pallas kernels for 0%

profile of v1, /device:TPU:1, one launch (start us, length us, event | category | flops | bytes accessed | tf_op | source)
XLA Modules:
  0.0 180.5 jit_solution(9861886903022652456)
XLA Ops:
  6.5 0.0 copy-start
  6.5 0.0 copy-start.3
  6.5 0.0 copy-start.2
  6.5 0.0 copy-start.4
  6.5 2.3 %copy.12 = bf16[2,32,64,128]{3,2,0,1:T(8,128)(2,1)} copy(bf16[2,32,64,128]{3,2,1,0:T(8,128)(2,1)} %param.16) | data formatting | bytes 2097152 | tf_op args[6]
  8.9 11.9 %all-to-all-start = ((bf16[2,32,64,128]{3,2,0,1:T(8,128)(2,1)}), bf16[2,32,64,128]{3,2,0,1:T(8,128)(2,1)S(1)}, u32[]{:S(2)}, u32[]{:S(2)}) async-start(bf16[2,32,64,128]{3,2,0,1:T(8,128)(2,1)} %copy.12), calls=%async_computation | async-start | bytes 2097152 | tf_op jit(solution)/shard_map/all_to_all | solution.py:257
  20.8 0.0 all-reduce.3.cloned.1.call-start
  20.8 0.0 copy-done.3
  20.8 0.0 copy-done.2
  20.9 0.0 copy-done
  20.9 0.7 gather_fusion
  21.6 25.3 %all-to-all-done = bf16[2,32,64,128]{3,2,0,1:T(8,128)(2,1)S(1)} async-done(((bf16[2,32,64,128]{3,2,0,1:T(8,128)(2,1)}), bf16[2,32,64,128]{3,2,0,1:T(8,128)(2,1)S(1)}, u32[]{:S(2)}, u32[]{:S(2)}) %all-to-all-start) | async-done | bytes 1048608 | tf_op jit(solution)/shard_map/all_to_all | solution.py:257
  47.0 0.6 gather_fusion.1
  47.6 0.1 fusion
  47.7 21.2 %all_to_all.30 = bf16[32,1,64,128]{3,2,1,0:T(8,128)(2,1)} all-to-all(bf16[32,1,64,128]{3,2,1,0:T(8,128)(2,1)S(1)} %fusion), channel_id=1, replica_groups=mesh['dp'=32,'seq'=2,'tensor'=4] {'dp'}, dimensions={0} | all-to-all | bytes 1048576 | tf_op jit(solution)/shard_map/all_to_all | solution.py:263
  68.9 0.0 all-reduce.3.cloned.1.call-update
  69.0 0.0 copy-done.4
  69.0 0.5 pad_bitcast_fusion.gain_ref
  69.5 29.3 %all-reduce.3.cloned.1.call-done.s0_ref = bf16[2048,128]{1,0:T(8,128)(2,1)} async-done(((bf16[2048,128]{1,0:T(8,128)(2,1)}), bf16[2048,128]{1,0:T(8,128)(2,1)}) %all-reduce.3.cloned.1.call-update) | async-done | bytes 524304 | tf_op jit(solution)/shard_map/psum | solution.py:265
  98.8 70.3 %scan_and_send.1.in_ref = bf16[256,8192]{1,0:T(8,128)(2,1)} custom-call(bf16[1024,2048]{1,0:T(8,128)(2,1)} %bitcast.37, bf16[1024,128]{1,0:T(8,128)(2,1)} %bitcast.40, bf16[1024,128]{1,0:T(8,128)(2,1)} %bitcast.41, f32[32,1024]{1,0:T(8,128)} %bitcast.42, f32[32,1024]{1,0:T(8,128)} %bitcast.43, f32[1,128]{1,0:T(1,128)} %pad_bitcast_fusion.gain_ref, ...), custom_call_target="tpu_custom_call" | custom-call | tf_op jit(solution)/shard_map/scan_and_send/pallas_call | solution.py:289
  169.1 0.0 copy-start.1
  169.1 2.2 %copy-done.1 = bf16[256,8192]{1,0:T(8,128)(2,1)S(1)} copy-done((bf16[256,8192]{1,0:T(8,128)(2,1)S(1)}, bf16[256,8192]{1,0:T(8,128)(2,1)}, u32[]{:S(2)}) %copy-start.1) | copy-done | bytes 4194328
  171.3 2.4 %place_result.1 = bf16[256,8192]{1,0:T(8,128)(2,1)} custom-call(bf16[256,8192]{1,0:T(8,128)(2,1)S(1)} %copy-done.1), custom_call_target="tpu_custom_call" | custom-call | tf_op jit(solution)/shard_map/place_result/pallas_call | solution.py:328
  (5 shorter events, 0.1 us)
Async XLA Ops:
  6.5 14.3 %copy-start = (s32[128]{0:T(128)S(1)}, s32[128]{0:T(128)}, u32[]{:S(2)}) copy-start(s32[128]{0:T(128)} %param.19) | copy-start | bytes 1540
  6.5 14.3 %copy-start.3 = (s32[32]{0:T(128)S(1)}, s32[32]{0:T(128)}, u32[]{:S(2)}) copy-start(s32[32]{0:T(128)} %param.18) | copy-start | bytes 388
  6.5 14.3 %copy-start.2 = (s32[32]{0:T(128)S(1)}, s32[32]{0:T(128)}, u32[]{:S(2)}) copy-start(s32[32]{0:T(128)} %param.17) | copy-start | bytes 388
  6.5 62.4 %copy-start.4 = (f32[32]{0:T(128)S(1)}, f32[32]{0:T(128)}, u32[]{:S(2)}) copy-start(f32[32]{0:T(128)} %param.15) | copy-start | bytes 388
  8.9 38.1 %all-to-all-start = ((bf16[2,32,64,128]{3,2,0,1:T(8,128)(2,1)}), bf16[2,32,64,128]{3,2,0,1:T(8,128)(2,1)S(1)}, u32[]{:S(2)}, u32[]{:S(2)}) async-start(bf16[2,32,64,128]{3,2,0,1:T(8,128)(2,1)} %copy.12), calls=%async_computation | async-start | bytes 2097152 | tf_op jit(solution)/shard_map/all_to_all | solution.py:257
  20.8 78.0 %all-reduce.3.cloned.1.call-start = ((), (), s32[]{:S(2)}) async-start(), calls=%async_computation.2 | async-start | bytes 1048576 | tf_op jit(solution)/shard_map/psum | solution.py:265
  169.1 2.2 %copy-start.1 = (bf16[256,8192]{1,0:T(8,128)(2,1)S(1)}, bf16[256,8192]{1,0:T(8,128)(2,1)}, u32[]{:S(2)}) copy-start(bf16[256,8192]{1,0:T(8,128)(2,1)} %scan_and_send.1.in_ref) | copy-start | bytes 12582916
Sparse Core Ops, SparseCore 0:
  69.1 29.6 all-reduce.2

commit v2 on v1

--- a/solution.py
+++ b/solution.py
@@ -12,6 +12,8 @@
 BLOCK = 128
 CHUNK = 8 * HEAD_DIM
 LOG2E = 1.4426950408889634
+ROW = 4
+SPAN = 4
 MESH = pl.DeviceIdType.MESH
 F32 = jnp.float32
 BF16 = jnp.bfloat16
@@ -44,7 +46,7 @@
         )
         sm[at, :] = jnp.where(row >= col, scores, 0.0)
         bt[at, :] = inputs.astype(F32).T
-    stacked = jnp.concatenate(ends + [gain_ref[...]], axis=0)
+    stacked = jnp.concatenate(ends, axis=0)
     pad = (-stacked.shape[0]) % 8
     if pad:
         stacked = jnp.concatenate([stacked, jnp.zeros((pad, BLOCK), F32)], axis=0)
@@ -52,13 +54,16 @@
     head = lax.broadcasted_iota(jnp.int32, (BLOCK, width), 1) // HEAD_DIM
     spread = (spot == head).astype(F32)
     wide = jnp.dot(stacked, spread, precision=lax.Precision.HIGHEST, preferred_element_type=F32)
+    gain = jnp.dot(
+        gain_ref[...], spread[:heads], precision=lax.Precision.HIGHEST, preferred_element_type=F32
+    )
     reach = jnp.zeros((1, width), F32)
     for b in range(blocks):
         end = wide[b : b + 1, :]
         rows_e[b] = jnp.broadcast_to(jnp.exp2(end), (8, width))
         rows_e[blocks + 1 + b] = jnp.broadcast_to(jnp.exp2(reach), (8, width))
         reach = reach + end
-    rows_e[blocks] = jnp.broadcast_to(wide[blocks : blocks + 1, :], (8, width))
+    rows_e[blocks] = jnp.broadcast_to(gain, (8, width))
     rows_e[2 * blocks + 1] = jnp.broadcast_to(jnp.exp2(reach), (8, width))
 
 
@@ -111,17 +116,37 @@
     summary[:, cols] = state[...].astype(BF16)
 
 
+def loop(start, stop, group, body):
+    def step(j, _):
+        for i in range(group):
+            body(start + j * group + i)
+        return 0
+
+    steps = (stop - start) // group
+    lax.fori_loop(0, steps, step, 0)
+    for i in range(start + steps * group, stop):
+        body(i)
+
+
 def kernel(
     blocks,
     ranks,
+    first_ref,
+    prefix_ref,
+    slot_ref,
+    x_hbm,
+    b_hbm,
+    c_hbm,
+    ld_hbm,
+    dt_hbm,
+    gain_ref,
+    snap_ref,
+    o_ref,
     x_ref,
     b_ref,
     c_ref,
     ld_ref,
     dt_ref,
-    gain_ref,
-    s0_ref,
-    o_ref,
     sm,
     bt,
     run_t,
@@ -135,60 +160,194 @@
     staged,
     sum_in,
     decay_in,
-    sib_send,
-    sib_recv,
+    begin,
+    spread,
+    held,
+    picked,
+    offered,
+    came,
+    place,
+    load_sem,
+    x_sem,
+    spread_send,
+    spread_recv,
+    pick_send,
+    pick_recv,
+    decay_sem,
+    sum_send,
+    sum_recv,
+    pass_send,
+    pass_recv,
     y_send,
     y_recv,
     own_sem,
 ):
     dp, core, y = lax.axis_index("dp"), lax.axis_index("seq"), lax.axis_index("tensor")
+    z, x = dp // ROW, dp % ROW
+    plane = lax.axis_size("dp")
+    rings = plane // ROW
     sibling = (dp, 1 - core, y)
     quarter = blocks * BLOCK // ranks
     width = x_ref.shape[1]
     chunks = width // CHUNK
+    piece = CHUNK // (SPAN * ROW)
 
     def peer(step):
         return (dp, core, lax.rem(y + step, ranks))
 
+    def chunk_of(k):
+        return pl.ds(pl.multiple_of(k * CHUNK, CHUNK), CHUNK)
+
+    def x_load(k):
+        cols = chunk_of(k)
+        return pltpu.make_async_copy(x_hbm.at[:, cols], x_ref.at[:, cols], x_sem.at[k])
+
     barrier = pltpu.get_barrier_semaphore()
-    pl.semaphore_signal(barrier, inc=1, device_id=sibling, device_id_type=MESH)
+
+    def greet(i):
+        who = (lax.rem(dp + i // 2, plane), lax.rem(core + i, 2), y)
+        pl.semaphore_signal(barrier, inc=1, device_id=who, device_id_type=MESH)
+
+    loop(1, 2 * plane, 9, greet)
     for step in range(1, ranks):
         pl.semaphore_signal(barrier, inc=1, device_id=peer(step), device_id_type=MESH)
-    pl.semaphore_wait(barrier, ranks)
-
-    prepare(blocks, b_ref, c_ref, ld_ref, dt_ref, gain_ref, sm, bt, run_t, urow, fac, rows_e)
-    decay_copy = pltpu.make_async_remote_copy(
-        src_ref=rows_e.at[2 * blocks + 1],
-        dst_ref=decay_in,
-        send_sem=sib_send.at[0],
-        recv_sem=sib_recv.at[0],
-        device_id=sibling,
-        device_id_type=MESH,
-    )
-    decay_copy.start()
-
-    def run_chunk(k, _):
-        local_chunk(
-            blocks, k, x_ref, c_ref, sm, bt, run_t, urow, fac, rows_e, state, summary, acc, growth
+
+    loads = [
+        pltpu.make_async_copy(src, dst, load_sem.at[i])
+        for i, (src, dst) in enumerate(
+            ((ld_hbm, ld_ref), (dt_hbm, dt_ref), (b_hbm, b_ref), (c_hbm, c_ref))
         )
-        return 0
-
-    lax.fori_loop(0, chunks, run_chunk, 0)
-    sum_copy = pltpu.make_async_remote_copy(
-        src_ref=summary,
-        dst_ref=sum_in,
-        send_sem=sib_send.at[1],
-        recv_sem=sib_recv.at[1],
-        device_id=sibling,
-        device_id_type=MESH,
-    )
-    sum_copy.start()
-    decay_copy.wait()
-    sum_copy.wait()
-    later = core == 1
+    ]
+    for load in loads:
+        load.start()
+    for k in range(chunks):
+        x_load(k).start()
+
+    @pl.when(core == 0)
+    def _():
+        sum_in[...] = jnp.zeros_like(sum_in)
+        decay_in[...] = jnp.ones_like(decay_in)
+
+    def decay_copy():
+        return pltpu.make_async_remote_copy(
+            src_ref=rows_e.at[2 * blocks + 1],
+            dst_ref=decay_in,
+            send_sem=decay_sem.at[0],
+            recv_sem=decay_sem.at[1],
+            device_id=sibling,
+            device_id_type=MESH,
+        )
+
+    def sum_copy(k):
+        return pltpu.make_async_remote_copy(
+            src_ref=summary.at[:, chunk_of(k)],
+            dst_ref=sum_in.at[:, chunk_of(k)],
+            send_sem=sum_send.at[k],
+            recv_sem=sum_recv.at[k],
+            device_id=sibling,
+            device_id_type=MESH,
+        )
+
+    def pass_copy(k):
+        return pltpu.make_async_remote_copy(
+            src_ref=begin.at[chunk_of(k)],
+            dst_ref=begin.at[chunk_of(k)],
+            send_sem=pass_send.at[k],
+            recv_sem=pass_recv.at[k],
+            device_id=sibling,
+            device_id_type=MESH,
+        )
+
+    def spread_out(k):
+        server, half = lax.rem(k, 2), k // 2
+
+        def refs(dz, dx):
+            q = dz + 1 + core
+            to_x = lax.rem(x + dx, ROW)
+            rows = pl.ds(pl.multiple_of(k * CHUNK + (q * ROW + to_x) * piece, piece), piece)
+            who = (lax.rem(z + dz + rings, rings) * ROW + to_x, server, y)
+            return snap_ref.at[:, rows], spread.at[half, q * ROW + x, pl.ds(2 * core, 2)], who
+
+        def send(src, dst, who):
+            pltpu.make_async_remote_copy(
+                src_ref=src,
+                dst_ref=dst,
+                send_sem=spread_send.at[k],
+                recv_sem=spread_recv.at[half],
+                device_id=who,
+                device_id_type=MESH,
+            ).start()
+
+        src, dst, who = refs(0, 0)
+
+        @pl.when(core == server)
+        def _():
+            pltpu.make_async_copy(src, dst, spread_recv.at[half]).start()
+
+        @pl.when(core != server)
+        def _():
+            send(src, dst, who)
+
+        def one(i):
+            dz = (lax.rem(i // ROW + 1, SPAN) - 1) * (1 - 2 * core)
+            send(*refs(dz, lax.rem(i, ROW)))
+
+        loop(1, SPAN * ROW, 5, one)
+
+    def slot_of(r):
+        return slot_ref[jnp.maximum(first_ref[r] + prefix_ref[r] - 1, 0)]
+
+    def locate(r):
+        slot = slot_of(r)
+        low = lax.rem(slot, 4)
+        q = lax.rem(z - slot // (4 * ROW) + 1 + low // 2 + rings, SPAN)
+        place[r] = (q * ROW + lax.rem(slot // 4, ROW)) * 4 + low
+
+    def pick(k):
+        server, half = lax.rem(k, 2), k // 2
+        here = spread.at[half]
+        pltpu.make_async_copy(here, here, spread_recv.at[half]).wait()
+        held[...] = here[...].reshape(held.shape)
+
+        def choose(i):
+            r = lax.rem(dp + i, plane)
+            picked[half, i] = held[place[r]]
+            return picked.at[half, i], offered.at[k, z, x], (r, 0, y)
+
+        def send(src, dst, who):
+            pltpu.make_async_remote_copy(
+                src_ref=src,
+                dst_ref=dst,
+                send_sem=pick_send.at[half],
+                recv_sem=pick_recv.at[k],
+                device_id=who,
+                device_id_type=MESH,
+            ).start()
+
+        loop(1, plane, 5, lambda i: send(*choose(i)))
+        src, dst, who = choose(0)
+
+        @pl.when(server == 0)
+        def _():
+            pltpu.make_async_copy(src, dst, pick_recv.at[k]).start()
+
+        @pl.when(server == 1)
+        def _():
+            send(src, dst, who)
+
+    def gather(k):
+        here = offered.at[k]
+        pltpu.make_async_copy(here, here, pick_recv.at[k]).wait()
+        came[...] = here[...]
+        slot = slot_of(dp)
+        low = lax.rem(slot, 4)
+        for q in range(SPAN):
+            at_z = lax.rem(slot // (4 * ROW) + q - 1 - low // 2 + rings, rings)
+            rows = pl.ds(pl.multiple_of(k * CHUNK + q * ROW * piece, ROW * piece), ROW * piece)
+            begin[rows, :] = came[at_z].reshape(ROW * piece, STATE)
 
     def y_copy(k, step):
-        cols = pl.ds(pl.multiple_of(k * CHUNK, CHUNK), CHUNK)
+        cols = chunk_of(k)
         there = pl.ds(pl.multiple_of(y * width + k * CHUNK, CHUNK), CHUNK)
         rows = pl.ds(pl.multiple_of(lax.rem(y + step, ranks) * quarter, quarter), quarter)
         if step == 0:
@@ -202,26 +361,108 @@
             device_id_type=MESH,
         )
 
-    def finish(k, _):
-        cols = pl.ds(pl.multiple_of(k * CHUNK, CHUNK), CHUNK)
-        decay = jnp.where(later, decay_in[0:1, cols], 1.0)
-        earlier = jnp.where(later, sum_in[:, cols].astype(F32), 0.0).astype(BF16)
-        begin = s0_ref[cols, :]
+    def finish(k):
+        @pl.when(core == 0)
+        def _():
+            gather(k)
+            pass_copy(k).start()
+
+        @pl.when(core == 1)
+        def _():
+            sum_copy(k).wait_recv()
+            pass_copy(k).wait_recv()
+
+        cols = chunk_of(k)
+        decay = decay_in[0:1, cols]
+        earlier = sum_in[:, cols]
+        first_state = begin[cols, :]
         for step in (2, 1, 3, 0):
             rows = pl.ds(pl.multiple_of(lax.rem(y + step, ranks) * quarter, quarter), quarter)
             c = c_ref[rows, :]
             mixed = decay * lax.dot_general(
-                c, begin, (((1,), (1,)), ((), ())), preferred_element_type=F32
+                c, first_state, (((1,), (1,)), ((), ())), preferred_element_type=F32
             ) + jnp.dot(c, earlier, preferred_element_type=F32)
             staged[rows, cols] = (acc[rows, cols] + growth[rows, cols] * mixed).astype(BF16)
             y_copy(k, step).start()
+
+    def stage(s, _):
+        @pl.when(s < chunks)
+        def _():
+            x_load(s).wait()
+            local_chunk(
+                blocks, s, x_ref, c_ref, sm, bt, run_t, urow, fac, rows_e, state, summary, acc, growth
+            )
+
+            @pl.when(core == 0)
+            def _():
+                sum_copy(s).start()
+
+            @pl.when(lax.rem(s, 2) == core)
+            def _():
+                pick(s)
+
+        @pl.when(s < chunks - 2)
+        def _():
+            spread_out(s + 2)
+
+        @pl.when(s >= 1)
+        def _():
+            finish(s - 1)
+
         return 0
 
-    lax.fori_loop(0, chunks, finish, 0)
+    pl.semaphore_wait(barrier, 2 * plane - 1 + ranks - 1)
+    spread_out(0)
+    for load in loads:
+        load.wait()
+    prepare(blocks, b_ref, c_ref, ld_ref, dt_ref, gain_ref, sm, bt, run_t, urow, fac, rows_e)
+    spread_out(1)
+
+    @pl.when(core == 0)
+    def _():
+        decay_copy().start()
+
+    loop(0, plane, 4, locate)
+
+    @pl.when(core == 1)
+    def _():
+        decay_copy().wait_recv()
+
+    lax.fori_loop(0, chunks + 1, stage, 0)
+
+    @pl.when(core == 0)
+    def _():
+        decay_copy().wait_send()
 
     def drain(k, _):
         for step in range(ranks):
             y_copy(k, step).wait()
+        server, half = lax.rem(k, 2), k // 2
+        pieces = picked.at[half]
+
+        @pl.when(core == server)
+        def _():
+            sent = pieces.at[pl.ds(0, plane - 2)]
+            pltpu.make_async_copy(sent, sent, spread_send.at[k]).wait()
+
+        @pl.when(core != server)
+        def _():
+            pltpu.make_async_copy(pieces, pieces, spread_send.at[k]).wait()
+
+        @pl.when(jnp.logical_and(core == 0, server == 0))
+        def _():
+            sent = pieces.at[pl.ds(0, plane - 1)]
+            pltpu.make_async_copy(sent, sent, pick_send.at[half]).wait()
+
+        @pl.when(jnp.logical_and(core == 1, server == 1))
+        def _():
+            pltpu.make_async_copy(pieces, pieces, pick_send.at[half]).wait()
+
+        @pl.when(core == 0)
+        def _():
+            sum_copy(k).wait_send()
+            pass_copy(k).wait_send()
+
         return 0
 
     lax.fori_loop(0, chunks, drain, 0)
@@ -248,21 +489,6 @@
         write.start()
     for write in writes:
         write.wait()
-
-
-def start_states(snapshots, first_snap, prefix_kilo, snap_slot):
-    slots_here, heads = snapshots.shape[:2]
-    row_size = 2 * slots_here
-    dp_count = lax.axis_size("dp")
-    spread = lax.all_to_all(snapshots, "dp", split_axis=1, concat_axis=0, tiled=True)
-    chosen = snap_slot[first_snap + prefix_kilo - 1]
-    within = chosen % row_size
-    mine = within // slots_here == lax.axis_index("seq")
-    picked = spread[(chosen // row_size) * slots_here + within % slots_here]
-    picked = jnp.where(mine[:, None, None, None], picked, jnp.zeros_like(picked))
-    got = lax.all_to_all(picked, "dp", split_axis=0, concat_axis=1, tiled=True)
-    del heads, dp_count
-    return lax.psum(got, "seq")[0]
 
 
 def per_device(
@@ -282,16 +508,22 @@
     blocks = length // BLOCK
     ranks = lax.axis_size("tensor")
     chunks = width // CHUNK
-    begin = start_states(snapshots, first_snap, prefix_kilo, snap_slot)
-    gain = jnp.pad(skip_gain, (0, BLOCK - heads)).reshape(1, BLOCK)
     out_shape = (length // ranks, width * ranks)
-    vmem = pl.BlockSpec(memory_space=pltpu.VMEM)
+    plane = lax.axis_size("dp")
+    piece = CHUNK // (SPAN * ROW)
+    hbm, smem = pl.BlockSpec(memory_space=pl.ANY), pl.BlockSpec(memory_space=pltpu.SMEM)
+    dma = pltpu.SemaphoreType.DMA
     mixed = pl.pallas_call(
         functools.partial(kernel, blocks, ranks),
         out_shape=jax.ShapeDtypeStruct(out_shape, BF16),
-        in_specs=[vmem] * 7,
-        out_specs=pl.BlockSpec(memory_space=pl.ANY),
+        in_specs=[smem] * 3 + [hbm] * 5 + [pl.BlockSpec(memory_space=pltpu.VMEM), hbm],
+        out_specs=hbm,
         scratch_shapes=[
+            pltpu.VMEM((length, width), BF16),
+            pltpu.VMEM((length, STATE), BF16),
+            pltpu.VMEM((length, STATE), BF16),
+            pltpu.VMEM((heads, length), F32),
+            pltpu.VMEM((heads, length), F32),
             pltpu.VMEM((length, BLOCK), F32),
             pltpu.VMEM((length, BLOCK), F32),
             pltpu.VMEM((length, BLOCK), F32),
@@ -305,24 +537,43 @@
             pltpu.VMEM((length, width), BF16),
             pltpu.VMEM((STATE, width), BF16),
             pltpu.VMEM((8, width), F32),
-            pltpu.SemaphoreType.DMA((2,)),
-            pltpu.SemaphoreType.DMA((2,)),
-            pltpu.SemaphoreType.DMA((chunks, ranks - 1)),
-            pltpu.SemaphoreType.DMA((chunks, ranks - 1)),
-            pltpu.SemaphoreType.DMA((chunks,)),
+            pltpu.VMEM((width, STATE), BF16),
+            pltpu.VMEM((chunks // 2, SPAN * ROW, 4, piece, STATE), BF16),
+            pltpu.VMEM((SPAN * ROW * 4, piece, STATE), BF16),
+            pltpu.VMEM((chunks // 2, plane, piece, STATE), BF16),
+            pltpu.VMEM((chunks, plane // ROW, ROW, piece, STATE), BF16),
+            pltpu.VMEM((plane // ROW, ROW, piece, STATE), BF16),
+            pltpu.SMEM((plane,), jnp.int32),
+            dma((4,)),
+            dma((chunks,)),
+            dma((chunks,)),
+            dma((chunks // 2,)),
+            dma((chunks // 2,)),
+            dma((chunks,)),
+            dma((2,)),
+            dma((chunks,)),
+            dma((chunks,)),
+            dma((chunks,)),
+            dma((chunks,)),
+            dma((chunks, ranks - 1)),
+            dma((chunks, ranks - 1)),
+            dma((chunks,)),
         ],
         compiler_params=pltpu.CompilerParams(
             collective_id=0, has_side_effects=True, vmem_limit_bytes=56 * 2**20
         ),
         name="scan_and_send",
     )(
+        first_snap,
+        prefix_kilo,
+        snap_slot,
         tokens[0],
         input_map[0],
         output_map[0],
         log_decay[0],
         step_size[0],
-        gain,
-        begin.reshape(width, STATE),
+        skip_gain.reshape(1, heads),
+        snapshots.reshape(snapshots.shape[0], width, STATE),
     )
     parts = 4
     result = pl.pallas_call(
@@ -335,7 +586,7 @@
             pltpu.SemaphoreType.DMA((parts,)),
             pltpu.SemaphoreType.DMA((parts,)),
         ],
-        compiler_params=pltpu.CompilerParams(vmem_limit_bytes=16 * 2**20),
+        compiler_params=pltpu.CompilerParams(vmem_limit_bytes=60 * 2**20),
         name="place_result",
     )(mixed)
     return result[None]

time: 181 us -> 81.5 us (0.45)
  waiting for transfers between devices: 54.6 us -> 0 us
  blocking collectives: 21.2 us -> 0 us
  between operations: 13.5 us -> 0.01 us
  starting transfers between devices: 11.9 us -> 0 us
  Pallas kernels: 72.7 us -> 81.4 us
  local copies, waits for them, and re-layouts: 6.4 us -> 0 us
    psum x1 -> x0, waiting for transfers between devices: 29.3 us -> none  [start_states(): return lax.psum(got, 'seq')[0]]
    all_to_all x1 -> x0, waiting for transfers between devices: 25.3 us -> none  [start_states(): lax.all_to_all(snapshots, 'dp', split_axis=1, concat_axis=0, tiled=True)]
    all_to_all x1 -> x0, blocking collectives: 21.2 us -> none  [start_states(): got = lax.all_to_all(picked, 'dp', split_axis=0, concat_axis=1, tiled=True)]
    all_to_all x1 -> x0, starting transfers between devices: 11.9 us -> none  [start_states(): lax.all_to_all(snapshots, 'dp', split_axis=1, concat_axis=0, tiled=True)]
    pallas_call x1, Pallas kernels: 70.3 us -> 78.1 us  [per_device(): pl.pallas_call(functools.partial(kernel, blocks, ranks), out_shape=jax.Sh...]
    unnamed x11 -> x0, local copies, waits for them, and re-layouts: 4.54 us -> none
  transfers between devices with their start and end apart: 2 -> 0, of which waited for: 2 -> 0; matrix products, arithmetic and copies ran while one was open for 1% -> 0% of each run, Pallas kernels for 0% -> 0%
where the time goes in v2:
time: 81.5 us; the launch traced here: 81.4 us
  Pallas kernels  81.4 us (100%)
    pallas_call x1, Pallas kernels, per_device(): pl.pallas_call(functools.partial(kernel, blocks, ranks), out_shape=jax.Sh...  78.1 us
    pallas_call x1, Pallas kernels, per_device(): pl.pallas_call(functools.partial(copy_kernel, parts), out_shape=jax.Shape...  3.3 us

profile of v2, /device:TPU:1, one launch (start us, length us, event | category | flops | bytes accessed | tf_op | source)
XLA Modules:
  0.0 81.4 jit_solution(2981160999241022714)
XLA Ops:
  0.0 78.1 %scan_and_send.1.in_ref = bf16[256,8192]{1,0:T(8,128)(2,1)} custom-call(s32[32]{0:T(128)} %first_ref.1, s32[32]{0:T(128)} %prefix_ref.1, s32[128]{0:T(128)} %slot_ref.1, bf16[1024,2048]{1,0:T(8,128)(2,1)} %bitcast.8, bf16[1024,128]{1,0:T(8,128)(2,1)} %bitcast.10, bf16[1024,128]{1,0:T(8,128)(2,1)} %bitcast.11, f32[32,1024]{1,0:T(8,128)} %bitcast.12, ...), custom_call_target="tpu_custom_call" | custom-call | tf_op jit(solution)/shard_map/scan_and_send/pallas_call | solution.py:516
  78.1 3.3 %place_result.1 = bf16[256,8192]{1,0:T(8,128)(2,1)} custom-call(bf16[256,8192]{1,0:T(8,128)(2,1)} %scan_and_send.1.in_ref), custom_call_target="tpu_custom_call" | custom-call | tf_op jit(solution)/shard_map/place_result/pallas_call | solution.py:579

commit v3 on v2

--- a/solution.py
+++ b/solution.py
@@ -19,13 +19,16 @@
 BF16 = jnp.bfloat16
 
 
-def prepare(blocks, b_ref, c_ref, ld_ref, dt_ref, gain_ref, sm, bt, run_t, urow, fac, rows_e):
+def prepare(
+    blocks, b_ref, c_ref, ld_ref, dt_ref, gain_ref, sm, bt, run_t, urow, fac, rows_e, reached
+):
     heads = ld_ref.shape[0]
     width = heads * HEAD_DIM
     row = lax.broadcasted_iota(jnp.int32, (BLOCK, BLOCK), 0)
     col = lax.broadcasted_iota(jnp.int32, (BLOCK, BLOCK), 1)
     upto = (row <= col).astype(F32)
     ends = []
+    so_far = jnp.zeros((heads, 1), F32)
     for b in range(blocks):
         at = pl.ds(b * BLOCK, BLOCK)
         run = jnp.dot(
@@ -36,6 +39,8 @@
         end = run[:, BLOCK - 1 :]
         urow[:, at] = run - jnp.log2(step)
         fac[:, at] = jnp.exp2(end - run) * step
+        reached[:, at] = jnp.exp2(run + so_far)
+        so_far = so_far + end
         padded = jnp.concatenate([run, jnp.zeros((BLOCK - heads, BLOCK), F32)], axis=0)
         turned = padded.T
         run_t[at, :] = turned
@@ -167,6 +172,12 @@
     offered,
     came,
     place,
+    reached,
+    entering,
+    early,
+    c_in,
+    decays_in,
+    state_in,
     load_sem,
     x_sem,
     spread_send,
@@ -181,6 +192,13 @@
     y_send,
     y_recv,
     own_sem,
+    map_send,
+    map_recv,
+    early_send,
+    early_recv,
+    state_send,
+    state_recv,
+    late_sem,
 ):
     dp, core, y = lax.axis_index("dp"), lax.axis_index("seq"), lax.axis_index("tensor")
     z, x = dp // ROW, dp % ROW
@@ -190,6 +208,7 @@
     quarter = blocks * BLOCK // ranks
     width = x_ref.shape[1]
     chunks = width // CHUNK
+    ahead = early.shape[0]
     piece = CHUNK // (SPAN * ROW)
 
     def peer(step):
@@ -361,6 +380,82 @@
             device_id_type=MESH,
         )
 
+    def map_copies(step):
+        rows = pl.ds(pl.multiple_of(lax.rem(y + step, ranks) * quarter, quarter), quarter)
+        pairs = ((c_ref.at[rows], c_in), (reached.at[pl.ds(0, ahead * 8), rows], decays_in))
+        return [
+            pltpu.make_async_remote_copy(
+                src_ref=src,
+                dst_ref=dst.at[step - 1],
+                send_sem=map_send.at[step - 1, i],
+                recv_sem=map_recv.at[step - 1, i],
+                device_id=peer(step),
+                device_id_type=MESH,
+            )
+            for i, (src, dst) in enumerate(pairs)
+        ]
+
+    def early_copy(k, step):
+        rows = pl.ds(pl.multiple_of(lax.rem(y + step, ranks) * quarter, quarter), quarter)
+        return pltpu.make_async_remote_copy(
+            src_ref=staged.at[rows, chunk_of(k)],
+            dst_ref=early.at[k, step - 1],
+            send_sem=early_send.at[k, step - 1],
+            recv_sem=early_recv.at[k, step - 1],
+            device_id=peer(step),
+            device_id_type=MESH,
+        )
+
+    def state_copy(k, step):
+        return pltpu.make_async_remote_copy(
+            src_ref=entering.at[:, chunk_of(k)],
+            dst_ref=state_in.at[k, step - 1],
+            send_sem=state_send.at[k, step - 1],
+            recv_sem=state_recv.at[k, step - 1],
+            device_id=peer(step),
+            device_id_type=MESH,
+        )
+
+    def late_copy(k, step):
+        whose = lax.rem(y + ranks - step, ranks)
+        there = pl.ds(pl.multiple_of(whose * width + k * CHUNK, CHUNK), CHUNK)
+        return pltpu.make_async_copy(
+            early.at[k, step - 1], o_ref.at[:, there], late_sem.at[k, step - 1]
+        )
+
+    def send_early(k):
+        cols = chunk_of(k)
+        for step in (2, 1, 3):
+            rows = pl.ds(pl.multiple_of(lax.rem(y + step, ranks) * quarter, quarter), quarter)
+            staged[rows, cols] = acc[rows, cols].astype(BF16)
+            early_copy(k, step).start()
+
+    def finish_late(k):
+        spot = lax.broadcasted_iota(jnp.int32, (BLOCK, CHUNK), 0)
+        head = lax.broadcasted_iota(jnp.int32, (BLOCK, CHUNK), 1) // HEAD_DIM + 8 * k
+        widen = (spot == head).astype(F32)
+        for step in (1, 3, 2):
+            early_copy(k, step).wait_recv()
+            state_copy(k, step).wait_recv()
+            entered = state_in[k, step - 1]
+            for half in range(quarter // BLOCK):
+                at = pl.ds(half * BLOCK, BLOCK)
+                decays = decays_in[step - 1, :, at]
+                padded = jnp.concatenate(
+                    [decays, jnp.zeros((BLOCK - decays.shape[0], BLOCK), F32)], axis=0
+                )
+                grown = jnp.dot(
+                    padded.T,
+                    widen,
+                    precision=lax.Precision.HIGHEST,
+                    preferred_element_type=F32,
+                )
+                mixed = jnp.dot(c_in[step - 1, at, :], entered, preferred_element_type=F32)
+                early[k, step - 1, at, :] = (
+                    early[k, step - 1, at, :].astype(F32) + grown * mixed
+                ).astype(BF16)
+            late_copy(k, step).start()
+
     def finish(k):
         @pl.when(core == 0)
         def _():
@@ -373,17 +468,31 @@
             pass_copy(k).wait_recv()
 
         cols = chunk_of(k)
-        decay = decay_in[0:1, cols]
-        earlier = sum_in[:, cols]
-        first_state = begin[cols, :]
-        for step in (2, 1, 3, 0):
+        for i in range(CHUNK // STATE):
+            part = pl.ds(pl.multiple_of(k * CHUNK + i * STATE, STATE), STATE)
+            loaded = begin[part, :].astype(F32).T
+            entering[:, part] = (
+                decay_in[0:1, part] * loaded + sum_in[:, part].astype(F32)
+            ).astype(BF16)
+        entered = entering[:, cols]
+
+        def output(step):
             rows = pl.ds(pl.multiple_of(lax.rem(y + step, ranks) * quarter, quarter), quarter)
-            c = c_ref[rows, :]
-            mixed = decay * lax.dot_general(
-                c, first_state, (((1,), (1,)), ((), ())), preferred_element_type=F32
-            ) + jnp.dot(c, earlier, preferred_element_type=F32)
+            mixed = jnp.dot(c_ref[rows, :], entered, preferred_element_type=F32)
             staged[rows, cols] = (acc[rows, cols] + growth[rows, cols] * mixed).astype(BF16)
             y_copy(k, step).start()
+
+        @pl.when(k < ahead)
+        def _():
+            for step in (2, 1, 3):
+                state_copy(k, step).start()
+
+        @pl.when(k >= ahead)
+        def _():
+            for step in (2, 1, 3):
+                output(step)
+
+        output(0)
 
     def stage(s, _):
         @pl.when(s < chunks)
@@ -393,6 +502,22 @@
                 blocks, s, x_ref, c_ref, sm, bt, run_t, urow, fac, rows_e, state, summary, acc, growth
             )
 
+            @pl.when(s < ahead)
+            def _():
+                send_early(s)
+
+            @pl.when(s == 0)
+            def _():
+                for step in (2, 1, 3):
+                    for copy in map_copies(step):
+                        copy.start()
+                spread_out(1)
+                loop(0, plane, 4, locate)
+
+                @pl.when(core == 1)
+                def _():
+                    decay_copy().wait_recv()
+
             @pl.when(core == 0)
             def _():
                 sum_copy(s).start()
@@ -411,32 +536,48 @@
 
         return 0
 
+    for load in loads:
+        load.wait()
+    prepare(
+        blocks, b_ref, c_ref, ld_ref, dt_ref, gain_ref, sm, bt, run_t, urow, fac, rows_e, reached
+    )
     pl.semaphore_wait(barrier, 2 * plane - 1 + ranks - 1)
     spread_out(0)
-    for load in loads:
-        load.wait()
-    prepare(blocks, b_ref, c_ref, ld_ref, dt_ref, gain_ref, sm, bt, run_t, urow, fac, rows_e)
-    spread_out(1)
 
     @pl.when(core == 0)
     def _():
         decay_copy().start()
 
-    loop(0, plane, 4, locate)
-
-    @pl.when(core == 1)
-    def _():
-        decay_copy().wait_recv()
-
     lax.fori_loop(0, chunks + 1, stage, 0)
+    for step in (1, 3, 2):
+        for copy in map_copies(step):
+            copy.wait()
+
+    def late(k, _):
+        finish_late(k)
+        return 0
+
+    lax.fori_loop(0, ahead, late, 0)
 
     @pl.when(core == 0)
     def _():
         decay_copy().wait_send()
 
     def drain(k, _):
-        for step in range(ranks):
-            y_copy(k, step).wait()
+        y_copy(k, 0).wait()
+
+        @pl.when(k < ahead)
+        def _():
+            for step in range(1, ranks):
+                early_copy(k, step).wait_send()
+                state_copy(k, step).wait_send()
+                late_copy(k, step).wait()
+
+        @pl.when(k >= ahead)
+        def _():
+            for step in range(1, ranks):
+                y_copy(k, step).wait()
+
         server, half = lax.rem(k, 2), k // 2
         pieces = picked.at[half]
 
@@ -511,6 +652,7 @@
     out_shape = (length // ranks, width * ranks)
     plane = lax.axis_size("dp")
     piece = CHUNK // (SPAN * ROW)
+    ahead = 1
     hbm, smem = pl.BlockSpec(memory_space=pl.ANY), pl.BlockSpec(memory_space=pltpu.SMEM)
     dma = pltpu.SemaphoreType.DMA
     mixed = pl.pallas_call(
@@ -544,6 +686,12 @@
             pltpu.VMEM((chunks, plane // ROW, ROW, piece, STATE), BF16),
             pltpu.VMEM((plane // ROW, ROW, piece, STATE), BF16),
             pltpu.SMEM((plane,), jnp.int32),
+            pltpu.VMEM((heads, length), F32),
+            pltpu.VMEM((STATE, width), BF16),
+            pltpu.VMEM((ahead, ranks - 1, length // ranks, CHUNK), BF16),
+            pltpu.VMEM((ranks - 1, length // ranks, STATE), BF16),
+            pltpu.VMEM((ranks - 1, ahead * 8, length // ranks), F32),
+            pltpu.VMEM((ahead, ranks - 1, STATE, CHUNK), BF16),
             dma((4,)),
             dma((chunks,)),
             dma((chunks,)),
@@ -558,6 +706,13 @@
             dma((chunks, ranks - 1)),
             dma((chunks, ranks - 1)),
             dma((chunks,)),
+            dma((ranks - 1, 2)),
+            dma((ranks - 1, 2)),
+            dma((ahead, ranks - 1)),
+            dma((ahead, ranks - 1)),
+            dma((ahead, ranks - 1)),
+            dma((ahead, ranks - 1)),
+            dma((ahead, ranks - 1)),
         ],
         compiler_params=pltpu.CompilerParams(
             collective_id=0, has_side_effects=True, vmem_limit_bytes=56 * 2**20

time: 81.5 us -> 77.5 us (0.951)
  Pallas kernels: 81.4 us -> 77.4 us
    pallas_call x1, Pallas kernels: 78.1 us -> 74.1 us  [per_device(): pl.pallas_call(functools.partial(kernel, blocks, ranks), out_shape=jax.Sh...]
where the time goes in v3:
time: 77.5 us; the launch traced here: 77.4 us
  Pallas kernels  77.4 us (100%)
    pallas_call x1, Pallas kernels, per_device(): pl.pallas_call(functools.partial(kernel, blocks, ranks), out_shape=jax.Sh...  74.1 us
    pallas_call x1, Pallas kernels, per_device(): pl.pallas_call(functools.partial(copy_kernel, parts), out_shape=jax.Shape...  3.3 us

profile of v3, /device:TPU:1, one launch (start us, length us, event | category | flops | bytes accessed | tf_op | source)
XLA Modules:
  0.0 77.4 jit_solution(8725329989274782966)
XLA Ops:
  0.0 74.1 %scan_and_send.1.in_ref = bf16[256,8192]{1,0:T(8,128)(2,1)} custom-call(s32[32]{0:T(128)} %first_ref.1, s32[32]{0:T(128)} %prefix_ref.1, s32[128]{0:T(128)} %slot_ref.1, bf16[1024,2048]{1,0:T(8,128)(2,1)} %bitcast.8, bf16[1024,128]{1,0:T(8,128)(2,1)} %bitcast.10, bf16[1024,128]{1,0:T(8,128)(2,1)} %bitcast.11, f32[32,1024]{1,0:T(8,128)} %bitcast.12, ...), custom_call_target="tpu_custom_call" | custom-call | tf_op jit(solution)/shard_map/scan_and_send/pallas_call | solution.py:658
  74.1 3.3 %place_result.1 = bf16[256,8192]{1,0:T(8,128)(2,1)} custom-call(bf16[256,8192]{1,0:T(8,128)(2,1)} %scan_and_send.1.in_ref), custom_call_target="tpu_custom_call" | custom-call | tf_op jit(solution)/shard_map/place_result/pallas_call | solution.py:734

commit v4 on v3

--- a/solution.py
+++ b/solution.py
@@ -14,6 +14,7 @@
 LOG2E = 1.4426950408889634
 ROW = 4
 SPAN = 4
+EARLY = 1
 MESH = pl.DeviceIdType.MESH
 F32 = jnp.float32
 BF16 = jnp.bfloat16
@@ -208,7 +209,6 @@
     quarter = blocks * BLOCK // ranks
     width = x_ref.shape[1]
     chunks = width // CHUNK
-    ahead = early.shape[0]
     piece = CHUNK // (SPAN * ROW)
 
     def peer(step):
@@ -239,7 +239,7 @@
     ]
     for load in loads:
         load.start()
-    for k in range(chunks):
+    for k in (EARLY, *(k for k in range(chunks) if k != EARLY)):
         x_load(k).start()
 
     @pl.when(core == 0)
@@ -311,7 +311,8 @@
             dz = (lax.rem(i // ROW + 1, SPAN) - 1) * (1 - 2 * core)
             send(*refs(dz, lax.rem(i, ROW)))
 
-        loop(1, SPAN * ROW, 5, one)
+        last = SPAN * ROW - 1
+        loop(0, last, 5, lambda i: one(lax.rem(i + 7, last) + 1))
 
     def slot_of(r):
         return slot_ref[jnp.maximum(first_ref[r] + prefix_ref[r] - 1, 0)]
@@ -329,9 +330,12 @@
         held[...] = here[...].reshape(held.shape)
 
         def choose(i):
-            r = lax.rem(dp + i, plane)
-            picked[half, i] = held[place[r]]
-            return picked.at[half, i], offered.at[k, z, x], (r, 0, y)
+            picked[half, i] = held[place[lax.rem(dp + i, plane)]]
+
+        loop(0, plane, 8, choose)
+
+        def refs(i):
+            return picked.at[half, i], offered.at[k, z, x], (lax.rem(dp + i, plane), 0, y)
 
         def send(src, dst, who):
             pltpu.make_async_remote_copy(
@@ -343,8 +347,9 @@
                 device_id_type=MESH,
             ).start()
 
-        loop(1, plane, 5, lambda i: send(*choose(i)))
-        src, dst, who = choose(0)
+        far = plane // 2 - 3
+        loop(0, plane - 1, 10, lambda i: send(*refs(lax.rem(i + far, plane - 1) + 1)))
+        src, dst, who = refs(0)
 
         @pl.when(server == 0)
         def _():
@@ -382,7 +387,7 @@
 
     def map_copies(step):
         rows = pl.ds(pl.multiple_of(lax.rem(y + step, ranks) * quarter, quarter), quarter)
-        pairs = ((c_ref.at[rows], c_in), (reached.at[pl.ds(0, ahead * 8), rows], decays_in))
+        pairs = ((c_ref.at[rows], c_in), (reached.at[pl.ds(EARLY * 8, 8), rows], decays_in))
         return [
             pltpu.make_async_remote_copy(
                 src_ref=src,
@@ -399,9 +404,9 @@
         rows = pl.ds(pl.multiple_of(lax.rem(y + step, ranks) * quarter, quarter), quarter)
         return pltpu.make_async_remote_copy(
             src_ref=staged.at[rows, chunk_of(k)],
-            dst_ref=early.at[k, step - 1],
-            send_sem=early_send.at[k, step - 1],
-            recv_sem=early_recv.at[k, step - 1],
+            dst_ref=early.at[step - 1],
+            send_sem=early_send.at[step - 1],
+            recv_sem=early_recv.at[step - 1],
             device_id=peer(step),
             device_id_type=MESH,
         )
@@ -409,9 +414,9 @@
     def state_copy(k, step):
         return pltpu.make_async_remote_copy(
             src_ref=entering.at[:, chunk_of(k)],
-            dst_ref=state_in.at[k, step - 1],
-            send_sem=state_send.at[k, step - 1],
-            recv_sem=state_recv.at[k, step - 1],
+            dst_ref=state_in.at[step - 1],
+            send_sem=state_send.at[step - 1],
+            recv_sem=state_recv.at[step - 1],
             device_id=peer(step),
             device_id_type=MESH,
         )
@@ -420,7 +425,7 @@
         whose = lax.rem(y + ranks - step, ranks)
         there = pl.ds(pl.multiple_of(whose * width + k * CHUNK, CHUNK), CHUNK)
         return pltpu.make_async_copy(
-            early.at[k, step - 1], o_ref.at[:, there], late_sem.at[k, step - 1]
+            early.at[step - 1], o_ref.at[:, there], late_sem.at[step - 1]
         )
 
     def send_early(k):
@@ -432,12 +437,12 @@
 
     def finish_late(k):
         spot = lax.broadcasted_iota(jnp.int32, (BLOCK, CHUNK), 0)
-        head = lax.broadcasted_iota(jnp.int32, (BLOCK, CHUNK), 1) // HEAD_DIM + 8 * k
+        head = lax.broadcasted_iota(jnp.int32, (BLOCK, CHUNK), 1) // HEAD_DIM
         widen = (spot == head).astype(F32)
         for step in (1, 3, 2):
             early_copy(k, step).wait_recv()
             state_copy(k, step).wait_recv()
-            entered = state_in[k, step - 1]
+            entered = state_in[step - 1]
             for half in range(quarter // BLOCK):
                 at = pl.ds(half * BLOCK, BLOCK)
                 decays = decays_in[step - 1, :, at]
@@ -451,8 +456,8 @@
                     preferred_element_type=F32,
                 )
                 mixed = jnp.dot(c_in[step - 1, at, :], entered, preferred_element_type=F32)
-                early[k, step - 1, at, :] = (
-                    early[k, step - 1, at, :].astype(F32) + grown * mixed
+                early[step - 1, at, :] = (
+                    early[step - 1, at, :].astype(F32) + grown * mixed
                 ).astype(BF16)
             late_copy(k, step).start()
 
@@ -482,50 +487,79 @@
             staged[rows, cols] = (acc[rows, cols] + growth[rows, cols] * mixed).astype(BF16)
             y_copy(k, step).start()
 
-        @pl.when(k < ahead)
+        @pl.when(k == EARLY)
         def _():
             for step in (2, 1, 3):
                 state_copy(k, step).start()
 
-        @pl.when(k >= ahead)
+        @pl.when(k != EARLY)
         def _():
             for step in (2, 1, 3):
                 output(step)
 
         output(0)
 
+    released_late = z >= rings // 4
+
+    def enter():
+        pl.semaphore_wait(barrier, 2 * plane - 1 + ranks - 1)
+        spread_out(0)
+
+        @pl.when(core == 0)
+        def _():
+            decay_copy().start()
+
     def stage(s, _):
+        scanned = jnp.where(s < 2, 1 - s, s)
+
         @pl.when(s < chunks)
         def _():
-            x_load(s).wait()
+            x_load(scanned).wait()
             local_chunk(
-                blocks, s, x_ref, c_ref, sm, bt, run_t, urow, fac, rows_e, state, summary, acc, growth
+                blocks,
+                scanned,
+                x_ref,
+                c_ref,
+                sm,
+                bt,
+                run_t,
+                urow,
+                fac,
+                rows_e,
+                state,
+                summary,
+                acc,
+                growth,
             )
 
-            @pl.when(s < ahead)
-            def _():
-                send_early(s)
-
-            @pl.when(s == 0)
-            def _():
-                for step in (2, 1, 3):
-                    for copy in map_copies(step):
-                        copy.start()
-                spread_out(1)
-                loop(0, plane, 4, locate)
-
-                @pl.when(core == 1)
-                def _():
-                    decay_copy().wait_recv()
-
+        @pl.when(s == 0)
+        def _():
+            pl.when(jnp.logical_not(released_late))(enter)
+            send_early(EARLY)
+            for step in (2, 1, 3):
+                for copy in map_copies(step):
+                    copy.start()
+
+        @pl.when(s < chunks)
+        def _():
             @pl.when(core == 0)
             def _():
-                sum_copy(s).start()
-
-            @pl.when(lax.rem(s, 2) == core)
+                sum_copy(scanned).start()
+
+            served = jnp.logical_and(s == 0, released_late)
+
+            @pl.when(jnp.logical_and(core == 0, jnp.logical_and(lax.rem(s, 2) == 0, jnp.logical_not(served))))
             def _():
                 pick(s)
 
+        @pl.when(s == 0)
+        def _():
+            spread_out(1)
+
+            @pl.when(core == 1)
+            def _():
+                decay_copy().wait_recv()
+
         @pl.when(s < chunks - 2)
         def _():
             spread_out(s + 2)
@@ -533,6 +567,10 @@
         @pl.when(s >= 1)
         def _():
             finish(s - 1)
+
+        @pl.when(jnp.logical_and(core == 1, jnp.logical_and(s < chunks, lax.rem(s, 2) == 1)))
+        def _():
+            pick(s)
 
         return 0
 
@@ -541,23 +579,19 @@
     prepare(
         blocks, b_ref, c_ref, ld_ref, dt_ref, gain_ref, sm, bt, run_t, urow, fac, rows_e, reached
     )
-    pl.semaphore_wait(barrier, 2 * plane - 1 + ranks - 1)
-    spread_out(0)
-
-    @pl.when(core == 0)
+    pl.when(released_late)(enter)
+    loop(0, plane, 4, locate)
+
+    @pl.when(jnp.logical_and(core == 0, released_late))
     def _():
-        decay_copy().start()
+        pick(0)
 
     lax.fori_loop(0, chunks + 1, stage, 0)
     for step in (1, 3, 2):
         for copy in map_copies(step):
             copy.wait()
 
-    def late(k, _):
-        finish_late(k)
-        return 0
-
-    lax.fori_loop(0, ahead, late, 0)
+    finish_late(EARLY)
 
     @pl.when(core == 0)
     def _():
@@ -566,14 +600,14 @@
     def drain(k, _):
         y_copy(k, 0).wait()
 
-        @pl.when(k < ahead)
+        @pl.when(k == EARLY)
         def _():
             for step in range(1, ranks):
                 early_copy(k, step).wait_send()
                 state_copy(k, step).wait_send()
                 late_copy(k, step).wait()
 
-        @pl.when(k >= ahead)
+        @pl.when(k != EARLY)
         def _():
             for step in range(1, ranks):
                 y_copy(k, step).wait()
@@ -652,7 +686,6 @@
     out_shape = (length // ranks, width * ranks)
     plane = lax.axis_size("dp")
     piece = CHUNK // (SPAN * ROW)
-    ahead = 1
     hbm, smem = pl.BlockSpec(memory_space=pl.ANY), pl.BlockSpec(memory_space=pltpu.SMEM)
     dma = pltpu.SemaphoreType.DMA
     mixed = pl.pallas_call(
@@ -688,10 +721,10 @@
             pltpu.SMEM((plane,), jnp.int32),
             pltpu.VMEM((heads, length), F32),
             pltpu.VMEM((STATE, width), BF16),
-            pltpu.VMEM((ahead, ranks - 1, length // ranks, CHUNK), BF16),
+            pltpu.VMEM((ranks - 1, length // ranks, CHUNK), BF16),
             pltpu.VMEM((ranks - 1, length // ranks, STATE), BF16),
-            pltpu.VMEM((ranks - 1, ahead * 8, length // ranks), F32),
-            pltpu.VMEM((ahead, ranks - 1, STATE, CHUNK), BF16),
+            pltpu.VMEM((ranks - 1, 8, length // ranks), F32),
+            pltpu.VMEM((ranks - 1, STATE, CHUNK), BF16),
             dma((4,)),
             dma((chunks,)),
             dma((chunks,)),
@@ -708,11 +741,11 @@
             dma((chunks,)),
             dma((ranks - 1, 2)),
             dma((ranks - 1, 2)),
-            dma((ahead, ranks - 1)),
-            dma((ahead, ranks - 1)),
-            dma((ahead, ranks - 1)),
-            dma((ahead, ranks - 1)),
-            dma((ahead, ranks - 1)),
+            dma((ranks - 1,)),
+            dma((ranks - 1,)),
+            dma((ranks - 1,)),
+            dma((ranks - 1,)),
+            dma((ranks - 1,)),
         ],
         compiler_params=pltpu.CompilerParams(
             collective_id=0, has_side_effects=True, vmem_limit_bytes=56 * 2**20

time: 77.5 us -> 76.6 us (0.988); the launches traced: 77.4 us -> 75.7 us
  Pallas kernels: 77.4 us -> 75.6 us
    pallas_call x1, Pallas kernels: 74.1 us -> 72.3 us  [per_device(): pl.pallas_call(functools.partial(kernel, blocks, ranks), out_shape=jax.Sh...]
where the time goes in v4:
time: 76.6 us; the launch traced here: 75.7 us
  Pallas kernels  75.6 us (99%)
    pallas_call x1, Pallas kernels, per_device(): pl.pallas_call(functools.partial(kernel, blocks, ranks), out_shape=jax.Sh...  72.3 us
    pallas_call x1, Pallas kernels, per_device(): pl.pallas_call(functools.partial(copy_kernel, parts), out_shape=jax.Shape...  3.3 us

profile of v4, /device:TPU:1, one launch (start us, length us, event | category | flops | bytes accessed | tf_op | source)
XLA Modules:
  0.0 75.7 jit_solution(1990438748161506078)
XLA Ops:
  0.0 72.3 %scan_and_send.1.in_ref = bf16[256,8192]{1,0:T(8,128)(2,1)} custom-call(s32[32]{0:T(128)} %first_ref.1, s32[32]{0:T(128)} %prefix_ref.1, s32[128]{0:T(128)} %slot_ref.1, bf16[1024,2048]{1,0:T(8,128)(2,1)} %bitcast.8, bf16[1024,128]{1,0:T(8,128)(2,1)} %bitcast.10, bf16[1024,128]{1,0:T(8,128)(2,1)} %bitcast.11, f32[32,1024]{1,0:T(8,128)} %bitcast.12, ...), custom_call_target="tpu_custom_call" | custom-call | tf_op jit(solution)/shard_map/scan_and_send/pallas_call | solution.py:691
  72.4 3.3 %place_result.1 = bf16[256,8192]{1,0:T(8,128)(2,1)} custom-call(bf16[256,8192]{1,0:T(8,128)(2,1)} %scan_and_send.1.in_ref), custom_call_target="tpu_custom_call" | custom-call | tf_op jit(solution)/shard_map/place_result/pallas_call | solution.py:767

commit v5 on v4

--- a/solution.py
+++ b/solution.py
@@ -118,7 +118,7 @@
             state[:, mine] = rows_e[b, :, here][0:1, :] * state[:, mine] + both[BLOCK:]
         return 0
 
-    lax.fori_loop(0, blocks, one, 0, unroll=2)
+    lax.fori_loop(0, blocks, one, 0, unroll=4)
     summary[:, cols] = state[...].astype(BF16)
 
 

time: 76.6 us -> 75.9 us (level)
  no operation moved by 1% of the time
where the time goes in v5:
time: 75.9 us; the launch traced here: 75.6 us
  Pallas kernels  75.6 us (100%)
    pallas_call x1, Pallas kernels, per_device(): pl.pallas_call(functools.partial(kernel, blocks, ranks), out_shape=jax.Sh...  72.3 us
    pallas_call x1, Pallas kernels, per_device(): pl.pallas_call(functools.partial(copy_kernel, parts), out_shape=jax.Shape...  3.3 us

profile of v5, /device:TPU:1, one launch (start us, length us, event | category | flops | bytes accessed | tf_op | source)
XLA Modules:
  0.0 75.6 jit_solution(1488053287316290479)
XLA Ops:
  0.0 72.3 %scan_and_send.1.in_ref = bf16[256,8192]{1,0:T(8,128)(2,1)} custom-call(s32[32]{0:T(128)} %first_ref.1, s32[32]{0:T(128)} %prefix_ref.1, s32[128]{0:T(128)} %slot_ref.1, bf16[1024,2048]{1,0:T(8,128)(2,1)} %bitcast.8, bf16[1024,128]{1,0:T(8,128)(2,1)} %bitcast.10, bf16[1024,128]{1,0:T(8,128)(2,1)} %bitcast.11, f32[32,1024]{1,0:T(8,128)} %bitcast.12, ...), custom_call_target="tpu_custom_call" | custom-call | tf_op jit(solution)/shard_map/scan_and_send/pallas_call | solution.py:691
  72.3 3.3 %place_result.1 = bf16[256,8192]{1,0:T(8,128)(2,1)} custom-call(bf16[256,8192]{1,0:T(8,128)(2,1)} %scan_and_send.1.in_ref), custom_call_target="tpu_custom_call" | custom-call | tf_op jit(solution)/shard_map/place_result/pallas_call | solution.py:767
